TPU v7x, 128 devices: a whole 4x4x4 slice. The times are simulated.
128 devices in a mesh: ep: 32 (over y_lo, z, x), rep: 4 (over y_hi, core).
Axes of the slice: x: 4, y: 4 (y_hi: 2, y_lo: 2; y = y_hi * 2 + y_lo), z: 4, core: 2. Of those that a mesh axis runs over, the one named last changes fastest.
Arguments:
- tokens: bfloat16 [4096, 4096], P('ep'), may hold values from -6 to 6
- out_grad: bfloat16 [4096, 4096], P('ep'), may hold values from -6 to 6
- expert_ids: int32 [4096, 8], P('ep'), may hold values from 0 to 15, all different within a row
- route_weights: float32 [4096, 8], P('ep'), may hold values from 0.05 to 0.6
- gate_up_weight: bfloat16 [32, 2, 768, 2048], P('ep', None, 'rep'), may hold values from -0.09375 to 0.09375
- down_weight: bfloat16 [32, 768, 2048], P('ep', 'rep'), may hold values from -0.21875 to 0.21875
- gate_up_m: float32 [32, 2, 768, 2048], P('ep', None, 'rep'), may hold values from -6 to 6
- gate_up_v: float32 [32, 2, 768, 2048], P('ep', None, 'rep'), may hold values from 1 to 100
- down_m: float32 [32, 768, 2048], P('ep', 'rep'), may hold values from -6 to 6
- down_v: float32 [32, 768, 2048], P('ep', 'rep'), may hold values from 1 to 100
Outputs:
- token_grad: bfloat16 [4096, 4096], P('ep', 'rep')
- new_gate_up: bfloat16 [32, 2, 768, 2048], P('ep', None, 'rep')
- new_down: bfloat16 [32, 768, 2048], P('ep', 'rep')
- new_gate_up_m: float32 [32, 2, 768, 2048], P('ep', None, 'rep')
- new_gate_up_v: float32 [32, 2, 768, 2048], P('ep', None, 'rep')
- new_down_m: float32 [32, 768, 2048], P('ep', 'rep')
- new_down_v: float32 [32, 768, 2048], P('ep', 'rep')
Inputs may be any that keep to these rules, and one draw needn't show every extreme that they name: `expert_ids`: each row names 8 different experts, and every expert is named by some row.
All inputs are finite; a program needn't handle non-finite values.
Results may differ from a plain program's by a relative error of at most 0.015.
Values may be sent and summed in bfloat16 or wider, within the bound.
No kernel may reach another device: no remote copies, remote signals or barrier semaphores. Data moves between devices by JAX's collectives and lax.ppermute only.
A program may use at most 192 MiB of HBM per device.

v0:
```python
import jax
import jax.numpy as jnp
from jax import lax
from jax.sharding import PartitionSpec as P

beta_first = 0.9
beta_second = 0.95
learn_rate = 0.01
decay_rate = 0.1
adam_epsilon = 1e-08
correct_first = 0.9999734386011124
correct_second = 0.994079470779666


def from_partner(value, axis, apart):
    mask = 2**apart
    pairs = [(source, source ^ mask) for source in range(lax.axis_size(axis))]
    return lax.ppermute(value, axis, pairs)


def contract(left, right, left_dim, right_dim):
    return lax.dot_general(
        left, right, (((left_dim,), (right_dim,)), ((), ())), preferred_element_type=jnp.float32
    )


def adam_step(weight, first, second, grad):
    first_new = beta_first * first + (1.0 - beta_first) * grad
    second_new = beta_second * second + (1.0 - beta_second) * grad * grad
    wide = weight.astype(jnp.float32)
    update = first_new / correct_first / (jnp.sqrt(second_new / correct_second) + adam_epsilon)
    return (
        (wide - learn_rate * (update + decay_rate * wide)).astype(jnp.bfloat16),
        first_new,
        second_new,
    )


def per_device(
    tokens,
    out_grad,
    expert_ids,
    route_weights,
    gate_up_weight,
    down_weight,
    gate_up_m,
    gate_up_v,
    down_m,
    down_v,
):
    ep_count = lax.axis_size("ep")
    tok_count, width = tokens.shape
    top_count = expert_ids.shape[1]
    expert_count = ep_count // 2
    slot_rows = tok_count * top_count // expert_count * 5 // 8
    route_count = tok_count * top_count
    row_count = ep_count * slot_rows
    flat_ids = expert_ids.reshape(route_count)
    onehot = (flat_ids[:, None] == jnp.arange(expert_count, dtype=jnp.int32)[None, :]).astype(
        jnp.int32
    )
    ranks = jnp.sum((jnp.cumsum(onehot, axis=0) - onehot) * onehot, axis=1)
    second_holder = (ranks >= slot_rows).astype(jnp.int32)
    target = (2 * flat_ids + second_holder) * slot_rows + ranks - second_holder * slot_rows
    target = jnp.where(ranks < 2 * slot_rows, target, -1)
    match = jnp.arange(row_count, dtype=jnp.int32)[:, None] == target[None, :]
    filled = jnp.any(match, axis=1)
    route_of_slot = jnp.sum(
        jnp.where(match, jnp.arange(route_count, dtype=jnp.int32)[None, :], 0), axis=1
    )
    token_of_slot = route_of_slot // top_count
    coeff = jnp.where(filled, route_weights.reshape(route_count)[route_of_slot], jnp.float32(0.0))
    send_x = jnp.where(filled[:, None], tokens[token_of_slot], jnp.zeros((), jnp.bfloat16))
    send_dy = (coeff[:, None] * out_grad[token_of_slot].astype(jnp.float32)).astype(jnp.bfloat16)
    send_x = send_x.reshape(ep_count, slot_rows, width)
    send_dy = send_dy.reshape(ep_count, slot_rows, width)
    got_x, got_dy = (
        lax.all_to_all(send_x, "ep", split_axis=0, concat_axis=0, tiled=True),
        lax.all_to_all(send_dy, "ep", split_axis=0, concat_axis=0, tiled=True),
    )
    row_x = got_x.reshape(row_count, width)
    row_dy = got_dy.reshape(row_count, width)
    low_first = lax.axis_index("ep") % 2 == 0
    other_gu, other_down = from_partner((gate_up_weight, down_weight), "ep", 0)
    full_gu = jnp.where(
        low_first,
        jnp.concatenate([gate_up_weight, other_gu], axis=3),
        jnp.concatenate([other_gu, gate_up_weight], axis=3),
    )[0]
    full_down = jnp.where(
        low_first,
        jnp.concatenate([down_weight, other_down], axis=2),
        jnp.concatenate([other_down, down_weight], axis=2),
    )[0]
    w_gate = full_gu[0]
    w_up = full_gu[1]
    gate = contract(row_x, w_gate, 1, 1)
    up = contract(row_x, w_up, 1, 1)
    sigma = jax.nn.sigmoid(gate)
    active = gate * sigma
    hidden = (active * up).astype(jnp.bfloat16)
    hidden_grad = contract(row_dy, full_down, 1, 1)
    up_grad = (hidden_grad * active).astype(jnp.bfloat16)
    gate_grad = (hidden_grad * up * sigma * (1.0 + gate * (1.0 - sigma))).astype(jnp.bfloat16)
    grad_down = contract(hidden, row_dy, 0, 0)
    grad_gate = contract(gate_grad, row_x, 0, 0)
    grad_up = contract(up_grad, row_x, 0, 0)
    partial_value = contract(gate_grad, w_gate, 1, 0) + contract(up_grad, w_up, 1, 0)
    half_rows = width // 2
    grad_gu = jnp.stack([grad_gate, grad_up])
    keep_gu = jnp.where(low_first, grad_gu[:, :, :half_rows], grad_gu[:, :, half_rows:])
    give_gu = jnp.where(low_first, grad_gu[:, :, half_rows:], grad_gu[:, :, :half_rows])
    keep_down = jnp.where(low_first, grad_down[:, :half_rows], grad_down[:, half_rows:])
    give_down = jnp.where(low_first, grad_down[:, half_rows:], grad_down[:, :half_rows])
    took_gu, took_down = (
        from_partner(give_gu.astype(jnp.bfloat16), "ep", 0).astype(give_gu.dtype),
        from_partner(give_down.astype(jnp.bfloat16), "ep", 0).astype(give_down.dtype),
    )
    total_gu = (keep_gu + took_gu)[None]
    total_down = (keep_down + took_down)[None]
    new_gu, gu_first, gu_second = adam_step(gate_up_weight, gate_up_m, gate_up_v, total_gu)
    new_down, down_first, down_second = adam_step(down_weight, down_m, down_v, total_down)
    rounded = partial_value.astype(jnp.bfloat16)
    pick = (token_of_slot[None, :] == jnp.arange(tok_count, dtype=jnp.int32)[:, None]) & filled[
        None, :
    ]
    back = lax.all_to_all(
        rounded.reshape(ep_count, slot_rows, width), "ep", split_axis=0, concat_axis=0, tiled=True
    ).reshape(row_count, width)
    token_sum = jnp.dot(pick.astype(jnp.bfloat16), back, preferred_element_type=jnp.float32)
    token_grad = lax.psum_scatter(
        token_sum.astype(jnp.bfloat16), "rep", scatter_dimension=1, tiled=True
    )
    return (token_grad, new_gu, new_down, gu_first, gu_second, down_first, down_second)


def solution(mesh):
    in_specs = (
        P("ep", None),
        P("ep", None),
        P("ep", None),
        P("ep", None),
        P("ep", None, "rep", None),
        P("ep", "rep", None),
        P("ep", None, "rep", None),
        P("ep", None, "rep", None),
        P("ep", "rep", None),
        P("ep", "rep", None),
    )
    out_specs = (
        P("ep", "rep"),
        P("ep", None, "rep", None),
        P("ep", "rep", None),
        P("ep", None, "rep", None),
        P("ep", None, "rep", None),
        P("ep", "rep", None),
        P("ep", "rep", None),
    )
    return jax.shard_map(
        per_device, mesh=mesh, in_specs=in_specs, out_specs=out_specs, check_vma=False
    )
```

profile of v0, /device:TPU:40, one launch (start us, length us, event | category | flops | bytes accessed | tf_op | source)
XLA Modules:
  0.0 653.0 jit_solution(16456293042294290451)
XLA Ops:
  14.7 8.2 %gather_fusion.2 = bf16[1280,4096]{1,0:T(8,128)(2,1)} fusion(bf16[128,4096]{1,0:T(8,128)(2,1)S(1)} %copy-done, s32[2048]{0:T(1024)S(1)} %get-tuple-element.17), kind=kCustom, calls=%fused_computation.2 | custom fusion | bytes 20976640 | tf_op jit(solution)/shard_map/gather | solution.py:73
  23.0 9.9 %broadcast_select_fusion = bf16[32,40,4096]{2,1,0:T(8,128)(2,1)} fusion(bf16[32,40,4096]{2,1,0:T(8,128)(2,1)} %bitcast.68, pred[32,40]{1,0:T(8,128)(4,1)S(1)} %reduce_or.12), kind=kLoop, calls=%fused_computation.6 | loop fusion | flops 5242880 | bytes 20972800 | tf_op jit(solution)/shard_map/jit(_where)/select_n | solution.py:73
  32.9 9.1 %all-to-all-start.1 = ((bf16[32,40,4096]{2,1,0:T(8,128)(2,1)}), bf16[32,40,4096]{2,1,0:T(8,128)(2,1)}, u32[]{:S(2)}, u32[]{:S(2)}) async-start(bf16[32,40,4096]{2,1,0:T(8,128)(2,1)} %broadcast_select_fusion), calls=%async_computation.1 | async-start | bytes 20971520 | tf_op jit(solution)/shard_map/all_to_all | solution.py:78
  42.3 5.0 gather_fusion
  47.3 8.3 %gather_fusion.1 = bf16[1280,4096]{1,0:T(8,128)(2,1)} fusion(bf16[128,4096]{1,0:T(8,128)(2,1)S(1)} %copy-done.2, s32[2048]{0:T(1024)S(1)} %get-tuple-element.17), kind=kCustom, calls=%fused_computation.1 | custom fusion | bytes 20976640 | tf_op jit(solution)/shard_map/gather | solution.py:74
  55.6 11.0 %fusion = bf16[32,40,4096]{2,1,0:T(8,128)(2,1)} fusion(bf16[32,40,4096]{2,1,0:T(8,128)(2,1)} %bitcast.67, f32[32,40]{1,0:T(8,128)S(1)} %broadcast_select_fusion.1), kind=kLoop, calls=%fused_computation.4 | loop fusion | flops 15728640 | bytes 20976640 | tf_op jit(solution)/shard_map/convert_element_type | solution.py:74
  66.6 123.6 %all-to-all-done.1 = bf16[32,40,4096]{2,1,0:T(8,128)(2,1)} async-done(((bf16[32,40,4096]{2,1,0:T(8,128)(2,1)}), bf16[32,40,4096]{2,1,0:T(8,128)(2,1)}, u32[]{:S(2)}, u32[]{:S(2)}) %all-to-all-start.1) | async-done | bytes 10485792 | tf_op jit(solution)/shard_map/all_to_all | solution.py:78
  190.2 19.7 %all-to-all-start = ((bf16[32,40,4096]{2,1,0:T(8,128)(2,1)}), bf16[32,40,4096]{2,1,0:T(8,128)(2,1)}, u32[]{:S(2)}, u32[]{:S(2)}) async-start(bf16[32,40,4096]{2,1,0:T(8,128)(2,1)} %fusion), calls=%async_computation | async-start | bytes 20971520 | tf_op jit(solution)/shard_map/all_to_all | solution.py:79
  212.0 177.1 %collective-permute-done.1 = bf16[1,2,192,2048]{3,2,1,0:T(8,128)(2,1)} collective-permute-done((bf16[1,2,192,2048]{3,2,1,0:T(8,128)(2,1)S(1)}, bf16[1,2,192,2048]{3,2,1,0:T(8,128)(2,1)}, u32[]{:S(2)}, u32[]{:S(2)}) %collective-permute-start.1) | collective-permute-done | bytes 1572896 | tf_op jit(solution)/shard_map/ppermute | solution.py:18
  392.1 9.6 %fusion.22 = f32[1280,192]{0,1:T(8,128)} fusion(bf16[1280,4096]{1,0:T(8,128)(2,1)} %bitcast.7, bf16[1,2,192,4096]{3,2,1,0:T(8,128)(2,1)S(1)} %maximum_select_fusion), kind=kOutput, calls=%fused_computation.52 | convolution fusion | flops 2013265920 | bytes 13041664 | tf_op jit(solution)/shard_map/dot_general | solution.py:22
  401.7 8.5 %fusion.20 = f32[1280,192]{0,1:T(8,128)} fusion(bf16[1280,4096]{1,0:T(8,128)(2,1)} %bitcast.7, bf16[1,2,192,4096]{3,2,1,0:T(8,128)(2,1)S(1)} %maximum_select_fusion), kind=kOutput, calls=%fused_computation.50 | convolution fusion | flops 2013265920 | bytes 13041664 | tf_op jit(solution)/shard_map/dot_general | solution.py:22
  411.1 8.8 %multiply_convert_fusion.1 = (bf16[1280,192]{0,1:T(8,128)(2,1)S(1)}, bf16[1280,192]{0,1:T(8,128)(2,1)S(1)}) fusion(f32[1280,192]{0,1:T(8,128)} %fusion.22, f32[1280,192]{0,1:T(8,128)} %fusion.20, bf16[1280,4096]{1,0:T(8,128)(2,1)} %bitcast.3, bf16[192,2048]{1,0:T(8,128)(2,1)} %bitcast.72, bf16[192,2048]{1,0:T(8,128)(2,1)S(1)} %bitcast.69, pred[]{:T(512)S(6)} %eq.70), kind=kOutput, calls=%fused_computation.54 | convolution fusion | flops 2023538688 | bytes 15007745 | tf_op jit(solution)/shard_map/dot_general | solution.py:22
  420.0 8.6 %fusion.21 = f32[1280,4096]{1,0:T(8,128)} fusion(bf16[1280,192]{0,1:T(8,128)(2,1)S(1)} %get-tuple-element.16, bf16[1,2,192,4096]{3,2,1,0:T(8,128)(2,1)S(1)} %copy-done.8), kind=kOutput, calls=%fused_computation.51 | convolution fusion | flops 2013265920 | bytes 23035904 | tf_op jit(solution)/shard_map/dot_general | solution.py:22
  428.5 12.4 %add_convert_fusion = bf16[1280,4096]{1,0:T(8,128)(2,1)} fusion(f32[1280,4096]{1,0:T(8,128)} %fusion.21, bf16[1280,192]{0,1:T(8,128)(2,1)S(1)} %get-tuple-element.15, bf16[1,2,192,4096]{3,2,1,0:T(8,128)(2,1)} %copy-done.7), kind=kOutput, calls=%fused_computation.5 | convolution fusion | flops 2023751680 | bytes 33521664 | tf_op jit(solution)/shard_map/dot_general | solution.py:22
  440.9 15.9 %all-to-all-start.2 = ((bf16[32,40,4096]{2,1,0:T(8,128)(2,1)}), bf16[32,40,4096]{2,1,0:T(8,128)(2,1)}, u32[]{:S(2)}, u32[]{:S(2)}) async-start(bf16[32,40,4096]{2,1,0:T(8,128)(2,1)} %bitcast.66), calls=%async_computation.2 | async-start | bytes 20971520 | tf_op jit(solution)/shard_map/all_to_all | solution.py:127
  457.1 6.8 %fusion.26 = f32[192,4096]{1,0:T(8,128)S(1)} fusion(bf16[1280,4096]{1,0:T(8,128)(2,1)} %bitcast.3, f32[1280,192]{0,1:T(8,128)} %fusion.20, f32[1280,192]{0,1:T(8,128)} %fusion.22), kind=kOutput, calls=%fused_computation.60 | convolution fusion | flops 2014740480 | bytes 15597568 | tf_op jit(solution)/shard_map/dot_general | solution.py:22
  467.4 6.2 convolution_bitcast_fusion
  473.6 7.3 %convolution_bitcast_fusion.1 = f32[1,192,4096]{2,1,0:T(8,128)S(1)} fusion(bf16[1280,192]{0,1:T(8,128)(2,1)S(1)} %get-tuple-element.16, bf16[1280,4096]{1,0:T(8,128)(2,1)} %bitcast.7), kind=kOutput, calls=%fused_computation.13 | convolution fusion | flops 2013265920 | bytes 14123008 | tf_op jit(solution)/shard_map/dot_general | solution.py:22
  483.7 107.9 %all-to-all-done.2 = bf16[32,40,4096]{2,1,0:T(8,128)(2,1)} async-done(((bf16[32,40,4096]{2,1,0:T(8,128)(2,1)}), bf16[32,40,4096]{2,1,0:T(8,128)(2,1)}, u32[]{:S(2)}, u32[]{:S(2)}) %all-to-all-start.2) | async-done | bytes 10485792 | tf_op jit(solution)/shard_map/all_to_all | solution.py:127
  591.6 6.5 convolution_convert_fusion
  598.2 10.3 %collective-permute-done.3 = bf16[192,2048]{1,0:T(8,128)(2,1)} collective-permute-done((bf16[192,2048]{1,0:T(8,128)(2,1)}, bf16[192,2048]{1,0:T(8,128)(2,1)}, u32[]{:S(2)}, u32[]{:S(2)}) %collective-permute-start.3) | collective-permute-done | bytes 786464 | tf_op jit(solution)/shard_map/ppermute | solution.py:18
  608.5 6.2 fusion.10
  614.7 24.9 %collective-permute-done.2 = bf16[2,192,2048]{2,1,0:T(8,128)(2,1)} collective-permute-done((bf16[2,192,2048]{2,1,0:T(8,128)(2,1)}, bf16[2,192,2048]{2,1,0:T(8,128)(2,1)}, u32[]{:S(2)}, u32[]{:S(2)}) %collective-permute-start.2) | collective-permute-done | bytes 1572896 | tf_op jit(solution)/shard_map/ppermute | solution.py:18
  639.6 6.5 %fusion.4 = (bf16[1,2,192,2048]{3,2,1,0:T(8,128)(2,1)}, f32[1,2,192,2048]{3,2,1,0:T(8,128)}, f32[1,2,192,2048]{3,2,1,0:T(8,128)}) fusion(bf16[1,2,192,2048]{3,2,1,0:T(8,128)(2,1)S(1)} %copy-done.10, f32[1,2,192,2048]{3,2,1,0:T(8,128)S(1)} %copy-done.11, f32[1,2,192,2048]{3,2,1,0:T(8,128)} %param.17, bf16[2,192,2048]{2,1,0:T(8,128)(2,1)} %collective-permute-done.2, ...), kind=kLoop, calls=%fused_computation.20 | loop fusion | flops 17301504 | bytes 23592960 | tf_op jit(solution)/shard_map/convert_element_type | solution.py:33
  (65 shorter events, 20.2 us)
Async XLA Ops:
  7.2 7.5 %copy-start = (bf16[128,4096]{1,0:T(8,128)(2,1)S(1)}, bf16[128,4096]{1,0:T(8,128)(2,1)}, u32[]{:S(2)}) copy-start(bf16[128,4096]{1,0:T(8,128)(2,1)} %param.10) | copy-start | bytes 3145732
  32.9 9.1 %copy-start.13 = (f32[128,8]{0,1:T(8,128)S(1)}, f32[128,8]{0,1:T(8,128)}, u32[]{:S(2)}) copy-start(f32[128,8]{0,1:T(8,128)} %param.13) | copy-start | bytes 12292
  32.9 157.3 %all-to-all-start.1 = ((bf16[32,40,4096]{2,1,0:T(8,128)(2,1)}), bf16[32,40,4096]{2,1,0:T(8,128)(2,1)}, u32[]{:S(2)}, u32[]{:S(2)}) async-start(bf16[32,40,4096]{2,1,0:T(8,128)(2,1)} %broadcast_select_fusion), calls=%async_computation.1 | async-start | bytes 20971520 | tf_op jit(solution)/shard_map/all_to_all | solution.py:78
  42.2 5.1 copy-start.2
  66.6 143.3 %copy-start.10 = (bf16[1,2,192,2048]{3,2,1,0:T(8,128)(2,1)S(1)}, bf16[1,2,192,2048]{3,2,1,0:T(8,128)(2,1)}, u32[]{:S(2)}) copy-start(bf16[1,2,192,2048]{3,2,1,0:T(8,128)(2,1)} %param.14) | copy-start | bytes 4718596
  66.6 144.8 %copy-start.12 = (bf16[1,192,2048]{2,1,0:T(8,128)(2,1)S(1)}, bf16[1,192,2048]{2,1,0:T(8,128)(2,1)}, u32[]{:S(2)}) copy-start(bf16[1,192,2048]{2,1,0:T(8,128)(2,1)} %param.15) | copy-start | bytes 2359300
  190.2 220.0 %all-to-all-start = ((bf16[32,40,4096]{2,1,0:T(8,128)(2,1)}), bf16[32,40,4096]{2,1,0:T(8,128)(2,1)}, u32[]{:S(2)}, u32[]{:S(2)}) async-start(bf16[32,40,4096]{2,1,0:T(8,128)(2,1)} %fusion), calls=%async_computation | async-start | bytes 20971520 | tf_op jit(solution)/shard_map/all_to_all | solution.py:79
  209.9 179.2 %collective-permute-start.1 = (bf16[1,2,192,2048]{3,2,1,0:T(8,128)(2,1)S(1)}, bf16[1,2,192,2048]{3,2,1,0:T(8,128)(2,1)}, u32[]{:S(2)}, u32[]{:S(2)}) collective-permute-start(bf16[1,2,192,2048]{3,2,1,0:T(8,128)(2,1)S(1)} %copy-done.10), channel_id=1, source_target_pairs={{0,4},{4,0},{8,12},{12,8},{16,20},{20,16},{24,28},{28,24},{32,36},... | collective-permute-start | bytes 4718600 | tf_op jit(solution)/shard_map/ppermute | solution.py:18
  211.5 198.8 %collective-permute-start = (bf16[1,192,2048]{2,1,0:T(8,128)(2,1)S(1)}, bf16[1,192,2048]{2,1,0:T(8,128)(2,1)S(1)}, u32[]{:S(2)}, u32[]{:S(2)}) collective-permute-start(bf16[1,192,2048]{2,1,0:T(8,128)(2,1)S(1)} %copy-done.12), channel_id=1, source_target_pairs={{0,4},{4,0},{8,12},{12,8},{16,20},{20,16},{24,28},{28,24},{32,36},... | collective-permute-start | bytes 2359304 | tf_op jit(solution)/shard_map/ppermute | solution.py:18
  392.1 9.7 %copy-start.7 = (bf16[1,2,192,4096]{3,2,1,0:T(8,128)(2,1)}, bf16[1,2,192,4096]{3,2,1,0:T(8,128)(2,1)S(1)}, u32[]{:S(2)}) copy-start(bf16[1,2,192,4096]{3,2,1,0:T(8,128)(2,1)S(1)} %maximum_select_fusion) | copy-start | bytes 9437188
  410.2 0.9 copy-start.14
  411.1 8.8 %copy-start.8 = (bf16[1,2,192,4096]{3,2,1,0:T(8,128)(2,1)S(1)}, bf16[1,2,192,4096]{3,2,1,0:T(8,128)(2,1)}, u32[]{:S(2)}) copy-start(bf16[1,2,192,4096]{3,2,1,0:T(8,128)(2,1)} %copy-done.7) | copy-start | bytes 9437188
  440.9 150.7 %all-to-all-start.2 = ((bf16[32,40,4096]{2,1,0:T(8,128)(2,1)}), bf16[32,40,4096]{2,1,0:T(8,128)(2,1)}, u32[]{:S(2)}, u32[]{:S(2)}) async-start(bf16[32,40,4096]{2,1,0:T(8,128)(2,1)} %bitcast.66), calls=%async_computation.2 | async-start | bytes 20971520 | tf_op jit(solution)/shard_map/all_to_all | solution.py:127
  456.8 189.3 %reduce-scatter.2.cloned.1.call-start = ((), (), s32[]{:S(2)}) async-start(), calls=%async_computation.4 | async-start | bytes 1310720 | tf_op jit(solution)/shard_map/reduce_scatter | solution.py:131
  464.0 2.0 copy-start.9
  466.0 142.5 %collective-permute-start.3 = (bf16[192,2048]{1,0:T(8,128)(2,1)}, bf16[192,2048]{1,0:T(8,128)(2,1)}, u32[]{:S(2)}, u32[]{:S(2)}) collective-permute-start(bf16[192,2048]{1,0:T(8,128)(2,1)} %select_convert_fusion.1), channel_id=1, source_target_pairs={{0,4},{4,0},{8,12},{12,8},{16,20},{20,16},{24,28},{28,24},{32,36},... | collective-permute-start | bytes 2359304 | tf_op jit(solution)/shard_map/ppermute | solution.py:18
  473.6 7.3 %copy-start.3 = (f32[1,192,4096]{2,1,0:T(8,128)}, f32[1,192,4096]{2,1,0:T(8,128)S(1)}, u32[]{:S(2)}) copy-start(f32[1,192,4096]{2,1,0:T(8,128)S(1)} %convolution_bitcast_fusion) | copy-start | bytes 9437188
  481.0 2.2 copy-start.5
  483.2 156.4 %collective-permute-start.2 = (bf16[2,192,2048]{2,1,0:T(8,128)(2,1)}, bf16[2,192,2048]{2,1,0:T(8,128)(2,1)}, u32[]{:S(2)}, u32[]{:S(2)}) collective-permute-start(bf16[2,192,2048]{2,1,0:T(8,128)(2,1)} %select_convert_fusion), channel_id=1, source_target_pairs={{0,4},{4,0},{8,12},{12,8},{16,20},{20,16},{24,28},{28,24},{32,36},... | collective-permute-start | bytes 4718600 | tf_op jit(solution)/shard_map/ppermute | solution.py:18
  598.1 41.5 %copy-start.4 = (f32[1,192,4096]{2,1,0:T(8,128)S(1)}, f32[1,192,4096]{2,1,0:T(8,128)}, u32[]{:S(2)}) copy-start(f32[1,192,4096]{2,1,0:T(8,128)} %copy-done.3) | copy-start | bytes 9437188
  598.1 41.5 %copy-start.6 = (f32[1,192,4096]{2,1,0:T(8,128)S(1)}, f32[1,192,4096]{2,1,0:T(8,128)}, u32[]{:S(2)}) copy-start(f32[1,192,4096]{2,1,0:T(8,128)} %copy-done.5) | copy-start | bytes 9437188
  598.2 41.4 %copy-start.11 = (f32[1,2,192,2048]{3,2,1,0:T(8,128)S(1)}, f32[1,2,192,2048]{3,2,1,0:T(8,128)}, u32[]{:S(2)}) copy-start(f32[1,2,192,2048]{3,2,1,0:T(8,128)} %param.16) | copy-start | bytes 9437188
  639.6 6.6 %copy-start.1 = (bf16[128,4096]{1,0:T(8,128)(2,1)S(1)}, bf16[128,4096]{1,0:T(8,128)(2,1)}, u32[]{:S(2)}) copy-start(bf16[128,4096]{1,0:T(8,128)(2,1)} %param.10) | copy-start | bytes 3145732
Sparse Core Ops, SparseCore 0:
  598.3 38.2 reduce-scatter.1
where the time goes:
time: 660 us; the launch traced here: 653 us
  waiting for transfers between devices  444 us (67%)
  matrix products  74.7 us (11%)
  starting transfers between devices  49.2 us (7%)
  other arithmetic  45.7 us (7%)
  local copies, waits for them, and re-layouts  25.3 us (4%)
  between operations  14.3 us (2%)
    ppermute x4, waiting for transfers between devices, from_partner(): return lax.ppermute(value, axis, pairs)  212 us
    all_to_all x1, waiting for transfers between devices, per_device(): lax.all_to_all(send_x, 'ep', split_axis=0, concat_axis=0, tiled=True)  124 us
    all_to_all x1, waiting for transfers between devices, per_device(): lax.all_to_all(rounded.reshape(ep_count, slot_rows, width), 'ep', split_a...  108 us
    dot_general x8, matrix products, contract(): lax.dot_general(left, right, (((left_dim,), (right_dim,)), ((), ())), pre...  68.2 us
    all_to_all x1, starting transfers between devices, per_device(): lax.all_to_all(send_dy, 'ep', split_axis=0, concat_axis=0, tiled=True)  19.7 us
    all_to_all x1, starting transfers between devices, per_device(): lax.all_to_all(rounded.reshape(ep_count, slot_rows, width), 'ep', split_a...  15.9 us
  transfers between devices with their start and end apart: 8, of which 5 were waited for; matrix products, arithmetic and copies ran while one was open for 14% of the time, Pallas kernels for 0%

commit v1 on v0

v1 whole, which is shorter than its diff:
```python
import functools

import jax
import jax.numpy as jnp
from jax import lax
from jax.experimental import pallas as pl
from jax.experimental.pallas import tpu as pltpu
from jax.sharding import PartitionSpec as P

beta_first = 0.9
beta_second = 0.95
learn_rate = 0.01
decay_rate = 0.1
adam_epsilon = 1e-08
correct_first = 0.9999734386011124
correct_second = 0.994079470779666

N_EP = 32
EXPERTS = 16
TOK = 128
TOP = 8
HALF_ROWS = 40
ROWS = N_EP * HALF_ROWS
QUARTER = 1024
HALF = 2048
HID = 192
F32 = jnp.float32
BF16 = jnp.bfloat16


def from_partner(value, axis, mask):
    pairs = [(source, source ^ mask) for source in range(lax.axis_size(axis))]
    return lax.ppermute(value, axis, pairs)


def exchange_groups():
    groups = []
    for core in range(2):
        for plane in range(2):
            members = []
            for ep in range(N_EP):
                y_hi = plane ^ (ep // 16) if core == 1 else plane
                members.append(ep * 4 + y_hi * 2 + core)
            groups.append(members)
    return groups


def exchange(value):
    return lax.all_to_all(
        value.reshape(N_EP, HALF_ROWS, QUARTER),
        ("ep", "rep"),
        split_axis=0,
        concat_axis=0,
        tiled=True,
        axis_index_groups=exchange_groups(),
    ).reshape(ROWS, QUARTER)


def contract(left, right, left_dim, right_dim):
    return lax.dot_general(
        left, right, (((left_dim,), (right_dim,)), ((), ())), preferred_element_type=F32
    )


def adam_step(weight, first, second, grad):
    first_new = beta_first * first + (1.0 - beta_first) * grad
    second_new = beta_second * second + (1.0 - beta_second) * grad * grad
    wide = weight.astype(F32)
    update = first_new / correct_first / (jnp.sqrt(second_new / correct_second) + adam_epsilon)
    return (
        (wide - learn_rate * (update + decay_rate * wide)).astype(BF16),
        first_new,
        second_new,
    )


def slot_match(place, ids_t):
    y_lo, y_hi, core = place[0], place[1], place[2]
    expert = lax.broadcasted_iota(jnp.int32, (EXPERTS, TOK), 0)
    named = jnp.zeros((EXPERTS, TOK), jnp.int32)
    for k in range(TOP):
        named += jnp.where(ids_t[k : k + 1, :] == expert, 1, 0)
    earlier = (
        lax.broadcasted_iota(jnp.int32, (TOK, TOK), 0)
        < lax.broadcasted_iota(jnp.int32, (TOK, TOK), 1)
    ).astype(F32)
    rank = contract(named.astype(F32).astype(BF16), earlier.astype(BF16), 1, 0)
    code = jnp.where(named > 0, rank, -1.0).astype(BF16)
    row = lax.broadcasted_iota(jnp.int32, (ROWS, EXPERTS), 0)
    low = lax.broadcasted_iota(jnp.int32, (ROWS, EXPERTS), 1) * (2 * HALF_ROWS)
    spread = jnp.where((row >= low) & (row < low + 2 * HALF_ROWS), 1.0, 0.0).astype(BF16)
    code_row = contract(spread, code, 1, 0)
    line = lax.broadcasted_iota(jnp.int32, (ROWS, TOK), 0)
    block = (line * 1639) >> 16
    flip = jnp.where(core == 1, 1, 0)
    half = y_hi ^ (flip & (y_lo ^ (block >> 4)))
    wanted = line - block * HALF_ROWS + half * HALF_ROWS
    match = code_row == wanted.astype(F32)
    return match, block & 1, spread


def pick_matrix(match, holder):
    low = jnp.where(match & (holder == 0), 1.0, 0.0)
    high = jnp.where(match & (holder == 1), 1.0, 0.0)
    return jnp.concatenate([low, high], axis=1).astype(BF16)


def send_tokens_kernel(place, ids_ref, low_ref, high_ref, out_ref, pick_ref):
    match, holder, _ = slot_match(place, ids_ref[...])
    pick = pick_matrix(match, holder)
    pick_ref[...] = pick
    out_ref[...] = (
        contract(pick[:, :TOK], low_ref[...], 1, 0) + contract(pick[:, TOK:], high_ref[...], 1, 0)
    ).astype(BF16)


def send_grads_kernel(place, ids_ref, weight_ref, low_ref, high_ref, out_ref):
    ids = ids_ref[...]
    match, holder, spread = slot_match(place, ids)
    pick = pick_matrix(match, holder)
    expert = lax.broadcasted_iota(jnp.int32, (EXPERTS, TOK), 0)
    weight = weight_ref[...]
    coeff = jnp.zeros((EXPERTS, TOK), F32)
    for k in range(TOP):
        coeff += jnp.where(ids[k : k + 1, :] == expert, weight[k : k + 1, :], 0.0)
    first = coeff.astype(BF16)
    rest = coeff - first.astype(F32)
    second = rest.astype(BF16)
    third = (rest - second.astype(F32)).astype(BF16)
    wide = (contract(spread, first, 1, 0) + contract(spread, second, 1, 0)) + contract(
        spread, third, 1, 0
    )
    scale = jnp.sum(jnp.where(match, wide, 0.0), axis=1, keepdims=True)
    rows = contract(pick[:, :TOK], low_ref[...], 1, 0) + contract(
        pick[:, TOK:], high_ref[...], 1, 0
    )
    out_ref[...] = (scale * rows).astype(BF16)


def quarter_spec(first):
    return pl.BlockSpec((TOK, QUARTER), lambda i, place: (0, first + place[2]))


def send_tokens(place, ids_t, tokens):
    return pl.pallas_call(
        send_tokens_kernel,
        out_shape=(
            jax.ShapeDtypeStruct((ROWS, QUARTER), BF16),
            jax.ShapeDtypeStruct((ROWS, 2 * TOK), BF16),
        ),
        grid_spec=pltpu.PrefetchScalarGridSpec(
            num_scalar_prefetch=1,
            grid=(1,),
            in_specs=[
                pl.BlockSpec((TOP, TOK), lambda i, place: (0, 0)),
                quarter_spec(0),
                quarter_spec(2),
            ],
            out_specs=(
                pl.BlockSpec((ROWS, QUARTER), lambda i, place: (0, 0)),
                pl.BlockSpec((ROWS, 2 * TOK), lambda i, place: (0, 0)),
            ),
        ),
        compiler_params=pltpu.CompilerParams(vmem_limit_bytes=48 * 1024 * 1024),
        cost_estimate=pl.CostEstimate(
            flops=2 * ROWS * 256 * QUARTER, bytes_accessed=4_000_000, transcendentals=0
        ),
        name="send_tokens",
    )(place, ids_t, tokens, tokens)


def send_grads(place, ids_t, weight_t, out_grad):
    return pl.pallas_call(
        send_grads_kernel,
        out_shape=jax.ShapeDtypeStruct((ROWS, QUARTER), BF16),
        grid_spec=pltpu.PrefetchScalarGridSpec(
            num_scalar_prefetch=1,
            grid=(1,),
            in_specs=[
                pl.BlockSpec((TOP, TOK), lambda i, place: (0, 0)),
                pl.BlockSpec((TOP, TOK), lambda i, place: (0, 0)),
                quarter_spec(0),
                quarter_spec(2),
            ],
            out_specs=pl.BlockSpec((ROWS, QUARTER), lambda i, place: (0, 0)),
        ),
        compiler_params=pltpu.CompilerParams(vmem_limit_bytes=48 * 1024 * 1024),
        cost_estimate=pl.CostEstimate(
            flops=2 * ROWS * 256 * QUARTER, bytes_accessed=4_000_000, transcendentals=0
        ),
        name="send_grads",
    )(place, ids_t, weight_t, out_grad, out_grad)


def trade_halves(received, core):
    mine = lax.dynamic_slice(received, (core * (ROWS // 2), 0), (ROWS // 2, QUARTER))
    give = lax.dynamic_slice(received, ((1 - core) * (ROWS // 2), 0), (ROWS // 2, QUARTER))
    took = from_partner(give, "rep", 1)
    return jnp.where(
        core == 0,
        jnp.concatenate([mine, took], axis=1),
        jnp.concatenate([took, mine], axis=1),
    )


def per_device(
    tokens,
    out_grad,
    expert_ids,
    route_weights,
    gate_up_weight,
    down_weight,
    gate_up_m,
    gate_up_v,
    down_m,
    down_v,
):
    ep = lax.axis_index("ep")
    rep = lax.axis_index("rep")
    y_hi = rep // 2
    core = rep % 2
    place = jnp.stack([ep // 16, y_hi, core]).astype(jnp.int32)
    ids_t = expert_ids.T
    weight_t = route_weights.T

    own_gu, own_down = gate_up_weight[0], down_weight[0]
    y_gu, y_down = from_partner(own_gu, "rep", 2), from_partner(own_down, "rep", 2)
    core_gu, core_down = from_partner(own_gu, "rep", 1), from_partner(own_down, "rep", 1)
    far_gu, far_down = from_partner(y_gu, "rep", 1), from_partner(y_down, "rep", 1)

    send_x, pick = send_tokens(place, ids_t, tokens)
    row_x = trade_halves(exchange(send_x), core)
    send_dy = send_grads(place, ids_t, weight_t, out_grad)
    row_dy = trade_halves(exchange(send_dy), core)

    w_gu = jnp.stack([own_gu, core_gu, y_gu, far_gu]).reshape(8 * HID, HALF)
    w_down = jnp.stack([own_down, core_down, y_down, far_down]).reshape(4 * HID, HALF)

    rows = ROWS // 2
    part_gu = contract(w_gu, row_x, 1, 1).astype(BF16)
    full_gu = part_gu.astype(F32) + from_partner(part_gu, "ep", 1).astype(F32)
    full_gu = full_gu.reshape(4, 2, HID, rows)
    part_hg = contract(w_down, row_dy, 1, 1).astype(BF16)
    hidden_grad = part_hg.astype(F32) + from_partner(part_hg, "ep", 1).astype(F32)
    hidden_grad = hidden_grad.reshape(4, HID, rows)

    gate, up = full_gu[:, 0], full_gu[:, 1]
    sigma = jax.nn.sigmoid(gate)
    active = gate * sigma
    hidden = (active * up).astype(BF16).reshape(4 * HID, rows)
    grad_down = contract(hidden, row_dy, 1, 0).reshape(4, HID, HALF)
    up_grad = (hidden_grad * active).astype(BF16)
    gate_grad = (hidden_grad * up * sigma * (1.0 + gate * (1.0 - sigma))).astype(BF16)
    grad_both = jnp.stack([gate_grad, up_grad], axis=1).reshape(8 * HID, rows)

    piece = contract(grad_both, w_gu, 0, 0).astype(BF16)
    lower, upper = piece[:, :QUARTER], piece[:, QUARTER:]
    keep = jnp.where(core == 0, lower, upper)
    give = jnp.where(core == 0, upper, lower)
    took = from_partner(give, "rep", 1)
    back = exchange(
        jnp.where(
            core == 0,
            jnp.concatenate([keep, took], axis=0),
            jnp.concatenate([took, keep], axis=0),
        )
    )

    grad_gu = contract(grad_both, row_x, 1, 0).reshape(4, 2, HID, HALF)

    def reduce_rep(grad):
        took = from_partner(jnp.stack([grad[1], grad[3]]).astype(BF16), "rep", 1).astype(F32)
        here = grad[0] + took[0]
        there = (grad[2] + took[1]).astype(BF16)
        return here, there

    here_down, there_down = reduce_rep(grad_down)
    here_gu, there_gu = reduce_rep(grad_gu)
    total_down = (here_down + from_partner(there_down, "rep", 2).astype(F32))[None]
    total_gu = (here_gu + from_partner(there_gu, "rep", 2).astype(F32))[None]
    new_gu, gu_first, gu_second = adam_step(gate_up_weight, gate_up_m, gate_up_v, total_gu)
    new_down, down_first, down_second = adam_step(down_weight, down_m, down_v, total_down)

    token_sum = contract(pick, back, 0, 0)
    lower, upper = token_sum[:TOK], token_sum[TOK:]
    keep = jnp.where(y_hi == 0, lower, upper)
    give = jnp.where(y_hi == 0, upper, lower).astype(BF16)
    token_grad = (keep + from_partner(give, "rep", 2).astype(F32)).astype(BF16)
    return (token_grad, new_gu, new_down, gu_first, gu_second, down_first, down_second)


def solution(mesh):
    in_specs = (
        P("ep", None),
        P("ep", None),
        P("ep", None),
        P("ep", None),
        P("ep", None, "rep", None),
        P("ep", "rep", None),
        P("ep", None, "rep", None),
        P("ep", None, "rep", None),
        P("ep", "rep", None),
        P("ep", "rep", None),
    )
    out_specs = (
        P("ep", "rep"),
        P("ep", None, "rep", None),
        P("ep", "rep", None),
        P("ep", None, "rep", None),
        P("ep", None, "rep", None),
        P("ep", "rep", None),
        P("ep", "rep", None),
    )
    return jax.shard_map(
        per_device, mesh=mesh, in_specs=in_specs, out_specs=out_specs, check_vma=False
    )
```

time: 660 us -> 322 us (0.49)
  waiting for transfers between devices: 444 us -> 179 us
  matrix products: 74.7 us -> 33.6 us
  between operations: 14.3 us -> 1.01 us
  local copies, waits for them, and re-layouts: 25.3 us -> 16.2 us
  other arithmetic: 45.7 us -> 37.8 us
  Pallas kernels: 0 us -> 6.89 us
    all_to_all x3, waiting for transfers between devices: 231 us -> 39 us  [exchange(): lax.all_to_all(value.reshape(N_EP, HALF_ROWS, QUARTER), ('ep', 'rep'), sp...]
    ppermute x4 -> x16, waiting for transfers between devices: 212 us -> 140 us  [from_partner(): return lax.ppermute(value, axis, pairs)]
    dot_general x8 -> x6, matrix products: 68.2 us -> 33.6 us  [contract(): lax.dot_general(left, right, (((left_dim,), (right_dim,)), ((), ())), pre...]
    gather x4 -> x0, local copies, waits for them, and re-layouts: 21.6 us -> none  [the longest x1 8.28 us: per_device(): out_grad[token_of_slot].astype(jnp.float32)]
    all_to_all x3, starting transfers between devices: 44.8 us -> 28.2 us  [exchange(): lax.all_to_all(value.reshape(N_EP, HALF_ROWS, QUARTER), ('ep', 'rep'), sp...]
    ppermute x4 -> x16, starting transfers between devices: 4.13 us -> 15.2 us  [from_partner(): return lax.ppermute(value, axis, pairs)]
    select_n x6 -> x2, other arithmetic: 12.9 us -> 2.74 us  [the longest x1 2.57 us: per_device(): jnp.where(core == 0, jnp.concatenate([keep, took], axis=0), jnp.concatena...]
    pallas_call x0 -> x2, Pallas kernels: none -> 6.89 us  [the longest x1 4.16 us: send_grads(): pl.pallas_call(send_grads_kernel, out_shape=jax.ShapeDtypeStruct((ROWS, Q...]
  transfers between devices with their start and end apart: 8 -> 19, of which waited for: 5 -> 7; matrix products, arithmetic and copies ran while one was open for 14% -> 21% of each run, Pallas kernels for 0% -> 1%
where the time goes in v1:
time: 322 us; the launch traced here: 318 us
  waiting for transfers between devices  179 us (56%)
  starting transfers between devices  43.4 us (13%)
  other arithmetic  37.8 us (12%)
  matrix products  33.6 us (10%)
  local copies, waits for them, and re-layouts  16.2 us (5%)
  Pallas kernels  6.89 us (2%)
    ppermute x16, waiting for transfers between devices, from_partner(): return lax.ppermute(value, axis, pairs)  140 us
    all_to_all x3, waiting for transfers between devices, exchange(): lax.all_to_all(value.reshape(N_EP, HALF_ROWS, QUARTER), ('ep', 'rep'), sp...  39 us
    dot_general x6, matrix products, contract(): lax.dot_general(left, right, (((left_dim,), (right_dim,)), ((), ())), pre...  33.6 us
    all_to_all x3, starting transfers between devices, exchange(): lax.all_to_all(value.reshape(N_EP, HALF_ROWS, QUARTER), ('ep', 'rep'), sp...  28.2 us
    ppermute x16, starting transfers between devices, from_partner(): return lax.ppermute(value, axis, pairs)  15.2 us
    convert_element_type x2, other arithmetic, adam_step(): (wide - learn_rate * (update + decay_rate * wide)).astype(BF16)  11.8 us
  transfers between devices with their start and end apart: 19, of which 7 were waited for; matrix products, arithmetic and copies ran while one was open for 21% of the time, Pallas kernels for 1%

profile of v1, /device:TPU:40, one launch (start us, length us, event | category | flops | bytes accessed | tf_op | source)
XLA Modules:
  0.0 318.1 jit_solution(16325444986081430117)
XLA Ops:
  2.7 2.7 send_tokens.1
  6.9 9.3 %all-to-all-start.1 = ((bf16[32,40,1024]{2,1,0:T(8,128)(2,1)}), bf16[32,40,1024]{2,1,0:T(8,128)(2,1)}, u32[]{:S(2)}, u32[]{:S(2)}) async-start(bf16[32,40,1024]{2,1,0:T(8,128)(2,1)} %bitcast.114), calls=%async_computation.1 | async-start | bytes 5242880 | tf_op jit(solution)/shard_map/all_to_all | solution.py:49
  18.6 4.2 %send_grads.1 = bf16[1280,1024]{1,0:T(8,128)(2,1)} custom-call(s32[3]{0:T(128)S(1)} %pad_add_fusion.place, s32[8,128]{1,0:T(8,128)S(1)} %bitcast.116, f32[8,128]{1,0:T(8,128)S(1)} %bitcast.117, bf16[128,4096]{1,0:T(8,128)(2,1)S(1)} %copy-done, bf16[128,4096]{1,0:T(8,128)(2,1)S(1)} %copy-done), custom_call_target="tpu_custom_call" | custom-call | flops 671088640 | bytes 4000000 | tf_op jit(solution)/shard_map/send_grads/pallas_call | solution.py:173
  22.7 26.2 %all-to-all-done.1 = bf16[32,40,1024]{2,1,0:T(8,128)(2,1)} async-done(((bf16[32,40,1024]{2,1,0:T(8,128)(2,1)}), bf16[32,40,1024]{2,1,0:T(8,128)(2,1)}, u32[]{:S(2)}, u32[]{:S(2)}) %all-to-all-start.1) | async-done | bytes 2621472 | tf_op jit(solution)/shard_map/all_to_all | solution.py:49
  48.9 9.8 %all-to-all-start = ((bf16[32,40,1024]{2,1,0:T(8,128)(2,1)}), bf16[32,40,1024]{2,1,0:T(8,128)(2,1)}, u32[]{:S(2)}, u32[]{:S(2)}) async-start(bf16[32,40,1024]{2,1,0:T(8,128)(2,1)} %bitcast.10), calls=%async_computation | async-start | bytes 5242880 | tf_op jit(solution)/shard_map/all_to_all | solution.py:49
  62.0 23.2 %collective-permute-done.6 = bf16[2,192,2048]{2,1,0:T(8,128)(2,1)} collective-permute-done((bf16[2,192,2048]{2,1,0:T(8,128)(2,1)S(1)}, bf16[2,192,2048]{2,1,0:T(8,128)(2,1)}, u32[]{:S(2)}, u32[]{:S(2)}) %collective-permute-start.6) | collective-permute-done | bytes 1572896 | tf_op jit(solution)/shard_map/ppermute | solution.py:33
  85.7 20.3 %collective-permute-done.1 = bf16[192,2048]{1,0:T(8,128)(2,1)} collective-permute-done((bf16[192,2048]{1,0:T(8,128)(2,1)S(1)}, bf16[192,2048]{1,0:T(8,128)(2,1)}, u32[]{:S(2)}, u32[]{:S(2)}) %collective-permute-start.1) | collective-permute-done | bytes 786464 | tf_op jit(solution)/shard_map/ppermute | solution.py:33
  106.0 3.4 %constant_dynamic-slice_fusion.1 = (bf16[640,1024]{1,0:T(8,128)(2,1)}, bf16[640,1024]{1,0:T(8,128)(2,1)}) fusion(bf16[1280,1024]{1,0:T(8,128)(2,1)} %bitcast.20, s32[]{:T(128)S(6)} %select_n.77, s32[]{:T(128)S(6)} %select_n.78), kind=kLoop, calls=%fused_computation.62 | loop fusion | bytes 5242888 | tf_op jit(solution)/shard_map/dynamic_slice | solution.py:196
  110.0 3.1 pad_maximum_fusion.1
  115.3 3.4 %pad_maximum_fusion = bf16[4,2,192,2048]{3,2,1,0:T(8,128)(2,1)S(1)} fusion(bf16[1,2,192,2048]{3,2,1,0:T(8,128)(2,1)} %bitcast.17, bf16[1,2,192,2048]{3,2,1,0:T(8,128)(2,1)} %bitcast.16, bf16[1,2,192,2048]{3,2,1,0:T(8,128)(2,1)} %bitcast.15, bf16[1,2,192,2048]{3,2,1,0:T(8,128)(2,1)S(1)} %copy-done.10), kind=kLoop, calls=%fused_computation | loop fusion | flops 9437184 | bytes 12582912 | tf_op jit(solution)/shard_map/stack | solution.py:236
  118.8 7.1 %convolution_convert_fusion = bf16[1536,640]{1,0:T(8,128)(2,1)S(1)} fusion(bf16[1536,2048]{1,0:T(8,128)(2,1)S(1)} %bitcast.126, bf16[640,1024]{1,0:T(8,128)(2,1)} %collective-permute-done.8, bf16[640,1024]{1,0:T(8,128)(2,1)S(1)} %copy-done.15, pred[]{:T(512)S(6)} %eq.7), kind=kOutput, calls=%fused_computation.6 | convolution fusion | flops 4039311360 | bytes 10878977 | tf_op jit(solution)/shard_map/dot_general | solution.py:60
  131.0 61.7 %collective-permute-done.4 = bf16[768,640]{1,0:T(8,128)(2,1)S(1)} collective-permute-done((bf16[768,640]{1,0:T(8,128)(2,1)S(1)}, bf16[768,640]{1,0:T(8,128)(2,1)S(1)}, u32[]{:S(2)}, u32[]{:S(2)}) %collective-permute-start.4) | collective-permute-done | bytes 983072 | tf_op jit(solution)/shard_map/ppermute | solution.py:33
  194.6 6.2 %bitcast_convert_fusion = bf16[640,2048]{1,0:T(8,128)(2,1)S(1)} fusion(bf16[4,1,192,640]{3,2,1,0:T(8,128)(2,1)S(1)} %get-tuple-element.22, bf16[4,1,192,640]{3,2,1,0:T(8,128)(2,1)S(1)} %get-tuple-element.21, bf16[1,2,192,2048]{3,2,1,0:T(8,128)(2,1)} %bitcast.17, bf16[1,2,192,2048]{3,2,1,0:T(8,128)(2,1)} %bitcast.16, bf16[1,2,192,2048]{3,2,1,0:T(8,128)(2,1)} %bitcast.15, ...), kind=kOutput, calls=%fused_computation.1 | convolution fusion | flops 4038262784 | bytes 10878976 | tf_op jit(solution)/shard_map/dot_general | solution.py:60
  201.5 10.0 %fusion.32 = (bf16[1536,2048]{1,0:T(8,128)(2,1)S(1)}, f32[1536,2048]{1,0:T(8,128)}) fusion(bf16[1536,640]{1,0:T(8,128)(2,1)S(1)} %bitcast.132, bf16[640,1024]{1,0:T(8,128)(2,1)} %collective-permute-done.8, bf16[640,1024]{1,0:T(8,128)(2,1)S(1)} %copy-done.15, pred[]{:T(512)S(6)} %eq.7), kind=kOutput, calls=%fused_computation.72 | convolution fusion | flops 4041474048 | bytes 23461888 | tf_op jit(solution)/shard_map/dot_general | solution.py:60
  215.2 4.9 %fusion.33 = (bf16[768,2048]{1,0:T(8,128)(2,1)S(1)}, f32[768,2048]{1,0:T(8,128)}) fusion(bf16[768,640]{1,0:T(8,128)(2,1)S(1)} %fusion.9, bf16[640,1024]{1,0:T(8,128)(2,1)S(1)} %copy-done.17, bf16[640,1024]{1,0:T(8,128)(2,1)S(1)} %get-tuple-element.31, pred[]{:T(512)S(6)} %eq.7), kind=kOutput, calls=%fused_computation.73 | convolution fusion | flops 2026635264 | bytes 13041665 | tf_op jit(solution)/shard_map/dot_general | solution.py:60
  224.5 9.2 %all-to-all-start.2 = ((bf16[32,40,1024]{2,1,0:T(8,128)(2,1)}), bf16[32,40,1024]{2,1,0:T(8,128)(2,1)}, u32[]{:S(2)}, u32[]{:S(2)}) async-start(bf16[32,40,1024]{2,1,0:T(8,128)(2,1)} %bitcast.25), calls=%async_computation.2 | async-start | bytes 5242880 | tf_op jit(solution)/shard_map/all_to_all | solution.py:49
  233.7 5.1 %fusion.30 = (f32[384,2048]{1,0:T(8,128)}, f32[384,2048]{1,0:T(8,128)S(1)}) fusion(f32[1536,2048]{1,0:T(8,128)} %get-tuple-element.34), kind=kLoop, calls=%fused_computation.70 | loop fusion | bytes 12582912 | tf_op jit(solution)/shard_map/slice | solution.py:273
  240.6 3.6 %fusion.19 = bf16[192,2048]{1,0:T(8,128)(2,1)} fusion(f32[2,192,2048]{2,1,0:T(8,128)S(1)} %convert_element_type.93, f32[768,2048]{1,0:T(8,128)} %get-tuple-element.36), kind=kLoop, calls=%fused_computation.46 | loop fusion | flops 786432 | bytes 3932160 | tf_op jit(solution)/shard_map/convert_element_type | solution.py:274
  250.2 3.5 %collective-permute-start.13 = (bf16[2,192,2048]{2,1,0:T(8,128)(2,1)}, bf16[2,192,2048]{2,1,0:T(8,128)(2,1)}, u32[]{:S(2)}, u32[]{:S(2)}) collective-permute-start(bf16[2,192,2048]{2,1,0:T(8,128)(2,1)} %fusion.6), channel_id=1, source_target_pairs={{0,2},{1,3},{2,0},{3,1},{4,6},{5,7},{6,4},{7,5},{8,10},{9,11},{10,... | collective-permute-start | bytes 4718600 | tf_op jit(solution)/shard_map/ppermute | solution.py:33
  253.7 12.8 %all-to-all-done.2 = bf16[32,40,1024]{2,1,0:T(8,128)(2,1)} async-done(((bf16[32,40,1024]{2,1,0:T(8,128)(2,1)}), bf16[32,40,1024]{2,1,0:T(8,128)(2,1)}, u32[]{:S(2)}, u32[]{:S(2)}) %all-to-all-start.2) | async-done | bytes 2621472 | tf_op jit(solution)/shard_map/all_to_all | solution.py:49
  266.5 2.8 fusion.34
  273.0 5.3 %fusion.15 = (bf16[1,192,2048]{2,1,0:T(8,128)(2,1)}, f32[1,192,2048]{2,1,0:T(8,128)}, f32[1,192,2048]{2,1,0:T(8,128)}) fusion(bf16[1,192,2048]{2,1,0:T(8,128)(2,1)S(1)} %copy-done.11, bf16[192,2048]{1,0:T(8,128)(2,1)} %collective-permute-done.15, f32[2,192,2048]{2,1,0:T(8,128)S(1)} %copy-done.8, f32[768,2048]{1,0:T(8,128)} %get-tuple-element.36, ...), kind=kLoop, calls=%fused_computation.41 | loop fusion | flops 7864320 | bytes 11796480 | tf_op jit(solution)/shard_map/convert_element_type | solution.py:71
  278.3 32.5 %collective-permute-done.11 = bf16[128,1024]{1,0:T(8,128)(2,1)S(1)} collective-permute-done((bf16[128,1024]{1,0:T(8,128)(2,1)S(1)}, bf16[128,1024]{1,0:T(8,128)(2,1)S(1)}, u32[]{:S(2)}, u32[]{:S(2)}) %collective-permute-start.11) | collective-permute-done | bytes 262176 | tf_op jit(solution)/shard_map/ppermute | solution.py:33
  311.7 6.4 %fusion.2 = (bf16[1,2,192,2048]{3,2,1,0:T(8,128)(2,1)}, f32[1,2,192,2048]{3,2,1,0:T(8,128)}, f32[1,2,192,2048]{3,2,1,0:T(8,128)}) fusion(bf16[1,2,192,2048]{3,2,1,0:T(8,128)(2,1)S(1)} %copy-done.10, bf16[2,192,2048]{2,1,0:T(8,128)(2,1)} %collective-permute-done.13, f32[2,192,2048]{2,1,0:T(8,128)S(1)} %bitcast.122, f32[2,2,192,2048]{3,2,1,0:T(8,128)S(1)} %bitcast.119, ...), kind=kLoop, calls=%fused_computation.9 | loop fusion | flops 15728640 | bytes 23592960 | tf_op jit(solution)/shard_map/convert_element_type | solution.py:71
  (88 shorter events, 40.4 us)
Async XLA Ops:
  6.9 11.7 %copy-start.4 = (f32[128,8]{0,1:T(8,128)S(1)}, f32[128,8]{0,1:T(8,128)}, u32[]{:S(2)}) copy-start(f32[128,8]{0,1:T(8,128)} %param.13) | copy-start | bytes 12292
  6.9 42.0 %all-to-all-start.1 = ((bf16[32,40,1024]{2,1,0:T(8,128)(2,1)}), bf16[32,40,1024]{2,1,0:T(8,128)(2,1)}, u32[]{:S(2)}, u32[]{:S(2)}) async-start(bf16[32,40,1024]{2,1,0:T(8,128)(2,1)} %bitcast.114), calls=%async_computation.1 | async-start | bytes 5242880 | tf_op jit(solution)/shard_map/all_to_all | solution.py:49
  16.2 69.0 %collective-permute-start.6 = (bf16[2,192,2048]{2,1,0:T(8,128)(2,1)S(1)}, bf16[2,192,2048]{2,1,0:T(8,128)(2,1)}, u32[]{:S(2)}, u32[]{:S(2)}) collective-permute-start(bf16[2,192,2048]{2,1,0:T(8,128)(2,1)S(1)} %bitcast.124), channel_id=1, source_target_pairs={{0,2},{1,3},{2,0},{3,1},{4,6},{5,7},{6,4},{7,5},{8,10},{9,11},{10,... | collective-permute-start | bytes 4718600 | tf_op jit(solution)/shard_map/ppermute | solution.py:33
  48.9 64.1 %all-to-all-start = ((bf16[32,40,1024]{2,1,0:T(8,128)(2,1)}), bf16[32,40,1024]{2,1,0:T(8,128)(2,1)}, u32[]{:S(2)}, u32[]{:S(2)}) async-start(bf16[32,40,1024]{2,1,0:T(8,128)(2,1)} %bitcast.10), calls=%async_computation | async-start | bytes 5242880 | tf_op jit(solution)/shard_map/all_to_all | solution.py:49
  58.7 47.3 %collective-permute-start.1 = (bf16[192,2048]{1,0:T(8,128)(2,1)S(1)}, bf16[192,2048]{1,0:T(8,128)(2,1)}, u32[]{:S(2)}, u32[]{:S(2)}) collective-permute-start(bf16[192,2048]{1,0:T(8,128)(2,1)S(1)} %bitcast.129), channel_id=1, source_target_pairs={{0,2},{1,3},{2,0},{3,1},{4,6},{5,7},{6,4},{7,5},{8,10},{9,11},{10,... | collective-permute-start | bytes 2359304 | tf_op jit(solution)/shard_map/ppermute | solution.py:33
  61.4 53.9 %collective-permute-start.5 = (bf16[2,192,2048]{2,1,0:T(8,128)(2,1)S(1)}, bf16[2,192,2048]{2,1,0:T(8,128)(2,1)}, u32[]{:S(2)}, u32[]{:S(2)}) collective-permute-start(bf16[2,192,2048]{2,1,0:T(8,128)(2,1)S(1)} %bitcast.125), channel_id=1, source_target_pairs={{0,1},{1,0},{2,3},{3,2},{4,5},{5,4},{6,7},{7,6},{8,9},{9,8},{10,11... | collective-permute-start | bytes 4718600 | tf_op jit(solution)/shard_map/ppermute | solution.py:33
  85.2 30.1 %collective-permute-start.7 = (bf16[2,192,2048]{2,1,0:T(8,128)(2,1)}, bf16[2,192,2048]{2,1,0:T(8,128)(2,1)}, u32[]{:S(2)}, u32[]{:S(2)}) collective-permute-start(bf16[2,192,2048]{2,1,0:T(8,128)(2,1)} %collective-permute-done.6), channel_id=1, source_target_pairs={{0,1},{1,0},{2,3},{3,2},{4,5},{5,4},{6,7},{7,6},{8,9},{9,8},{10,11... | collective-permute-start | bytes 4718600 | tf_op jit(solution)/shard_map/ppermute | solution.py:33
  85.2 24.8 %collective-permute-start = (bf16[192,2048]{1,0:T(8,128)(2,1)S(1)}, bf16[192,2048]{1,0:T(8,128)(2,1)}, u32[]{:S(2)}, u32[]{:S(2)}) collective-permute-start(bf16[192,2048]{1,0:T(8,128)(2,1)S(1)} %bitcast.130), channel_id=1, source_target_pairs={{0,1},{1,0},{2,3},{3,2},{4,5},{5,4},{6,7},{7,6},{8,9},{9,8},{10,11... | collective-permute-start | bytes 2359304 | tf_op jit(solution)/shard_map/ppermute | solution.py:33
  106.0 4.0 %collective-permute-start.2 = (bf16[192,2048]{1,0:T(8,128)(2,1)}, bf16[192,2048]{1,0:T(8,128)(2,1)}, u32[]{:S(2)}, u32[]{:S(2)}) collective-permute-start(bf16[192,2048]{1,0:T(8,128)(2,1)} %collective-permute-done.1), channel_id=1, source_target_pairs={{0,1},{1,0},{2,3},{3,2},{4,5},{5,4},{6,7},{7,6},{8,9},{9,8},{10,11... | collective-permute-start | bytes 2359304 | tf_op jit(solution)/shard_map/ppermute | solution.py:33
  109.4 9.3 %collective-permute-start.8 = (bf16[640,1024]{1,0:T(8,128)(2,1)}, bf16[640,1024]{1,0:T(8,128)(2,1)}, u32[]{:S(2)}, u32[]{:S(2)}) collective-permute-start(bf16[640,1024]{1,0:T(8,128)(2,1)} %get-tuple-element.30), channel_id=1, source_target_pairs={{0,1},{1,0},{2,3},{3,2},{4,5},{5,4},{6,7},{7,6},{8,9},{9,8},{10,11... | collective-permute-start | bytes 3932168 | tf_op jit(solution)/shard_map/ppermute | solution.py:33
  115.0 13.2 %collective-permute-start.3 = (bf16[640,1024]{1,0:T(8,128)(2,1)S(1)}, bf16[640,1024]{1,0:T(8,128)(2,1)S(1)}, u32[]{:S(2)}, u32[]{:S(2)}) collective-permute-start(bf16[640,1024]{1,0:T(8,128)(2,1)S(1)} %get-tuple-element.32), channel_id=1, source_target_pairs={{0,1},{1,0},{2,3},{3,2},{4,5},{5,4},{6,7},{7,6},{8,9},{9,8},{10,11... | collective-permute-start | bytes 3932168 | tf_op jit(solution)/shard_map/ppermute | solution.py:33
  125.9 67.1 %collective-permute-start.9 = (bf16[1536,640]{1,0:T(8,128)(2,1)S(1)}, bf16[1536,640]{1,0:T(8,128)(2,1)S(1)}, u32[]{:S(2)}, u32[]{:S(2)}) collective-permute-start(bf16[1536,640]{1,0:T(8,128)(2,1)S(1)} %convolution_convert_fusion), channel_id=1, source_target_pairs={{0,4},{4,0},{8,12},{12,8},{16,20},{20,16},{24,28},{28,24},{32,36},... | collective-permute-start | bytes 5898248 | tf_op jit(solution)/shard_map/ppermute | solution.py:33
  130.9 61.8 %collective-permute-start.4 = (bf16[768,640]{1,0:T(8,128)(2,1)S(1)}, bf16[768,640]{1,0:T(8,128)(2,1)S(1)}, u32[]{:S(2)}, u32[]{:S(2)}) collective-permute-start(bf16[768,640]{1,0:T(8,128)(2,1)S(1)} %convolution_convert_fusion.1), channel_id=1, source_target_pairs={{0,4},{4,0},{8,12},{12,8},{16,20},{20,16},{24,28},{28,24},{32,36},... | collective-permute-start | bytes 2949128 | tf_op jit(solution)/shard_map/ppermute | solution.py:33
  201.2 20.7 %collective-permute-start.10 = (bf16[640,1024]{1,0:T(8,128)(2,1)S(1)}, bf16[640,1024]{1,0:T(8,128)(2,1)S(1)}, u32[]{:S(2)}, u32[]{:S(2)}) collective-permute-start(bf16[640,1024]{1,0:T(8,128)(2,1)S(1)} %get-tuple-element.28), channel_id=1, source_target_pairs={{0,1},{1,0},{2,3},{3,2},{4,5},{5,4},{6,7},{7,6},{8,9},{9,8},{10,11... | collective-permute-start | bytes 3932168 | tf_op jit(solution)/shard_map/ppermute | solution.py:33
  213.8 30.4 %collective-permute-start.12 = (bf16[2,2,192,2048]{3,2,1,0:T(8,128)(2,1)}, bf16[2,2,192,2048]{3,2,1,0:T(8,128)(2,1)}, u32[]{:S(2)}, u32[]{:S(2)}) collective-permute-start(bf16[2,2,192,2048]{3,2,1,0:T(8,128)(2,1)} %pad_maximum_fusion.2), channel_id=1, source_target_pairs={{0,1},{1,0},{2,3},{3,2},{4,5},{5,4},{6,7},{7,6},{8,9},{9,8},{10,11... | collective-permute-start | bytes 9437192 | tf_op jit(solution)/shard_map/ppermute | solution.py:33
  221.5 17.3 %collective-permute-start.14 = (bf16[2,192,2048]{2,1,0:T(8,128)(2,1)}, bf16[2,192,2048]{2,1,0:T(8,128)(2,1)}, u32[]{:S(2)}, u32[]{:S(2)}) collective-permute-start(bf16[2,192,2048]{2,1,0:T(8,128)(2,1)} %pad_maximum_fusion.4), channel_id=1, source_target_pairs={{0,1},{1,0},{2,3},{3,2},{4,5},{5,4},{6,7},{7,6},{8,9},{9,8},{10,11... | collective-permute-start | bytes 4718600 | tf_op jit(solution)/shard_map/ppermute | solution.py:33
  224.5 42.0 %all-to-all-start.2 = ((bf16[32,40,1024]{2,1,0:T(8,128)(2,1)}), bf16[32,40,1024]{2,1,0:T(8,128)(2,1)}, u32[]{:S(2)}, u32[]{:S(2)}) async-start(bf16[32,40,1024]{2,1,0:T(8,128)(2,1)} %bitcast.25), calls=%async_computation.2 | async-start | bytes 5242880 | tf_op jit(solution)/shard_map/all_to_all | solution.py:49
  244.2 28.8 %collective-permute-start.15 = (bf16[192,2048]{1,0:T(8,128)(2,1)}, bf16[192,2048]{1,0:T(8,128)(2,1)}, u32[]{:S(2)}, u32[]{:S(2)}) collective-permute-start(bf16[192,2048]{1,0:T(8,128)(2,1)} %fusion.19), channel_id=1, source_target_pairs={{0,2},{1,3},{2,0},{3,1},{4,6},{5,7},{6,4},{7,5},{8,10},{9,11},{10,... | collective-permute-start | bytes 2359304 | tf_op jit(solution)/shard_map/ppermute | solution.py:33
  250.2 61.5 %collective-permute-start.13 = (bf16[2,192,2048]{2,1,0:T(8,128)(2,1)}, bf16[2,192,2048]{2,1,0:T(8,128)(2,1)}, u32[]{:S(2)}, u32[]{:S(2)}) collective-permute-start(bf16[2,192,2048]{2,1,0:T(8,128)(2,1)} %fusion.6), channel_id=1, source_target_pairs={{0,2},{1,3},{2,0},{3,1},{4,6},{5,7},{6,4},{7,5},{8,10},{9,11},{10,... | collective-permute-start | bytes 4718600 | tf_op jit(solution)/shard_map/ppermute | solution.py:33
  269.3 42.4 %slice-start = ((s8[6291456]{0:T(1024)(128)(4,1)}), s8[4194304]{0:T(1024)(128)(4,1)S(1)}, s32[]{:S(2)}) async-start(s8[6291456]{0:T(1024)(128)(4,1)} %bitcast.118), calls=%async_computation.3 | async-start | bytes 8388608
  269.3 42.4 %slice-start.1 = ((s8[6291456]{0:T(1024)(128)(4,1)}), s8[2097152]{0:T(1024)(128)(4,1)S(1)}, s32[]{:S(2)}) async-start(s8[6291456]{0:T(1024)(128)(4,1)} %bitcast.118), calls=%async_computation.4 | async-start | bytes 4194304
  269.3 41.5 %collective-permute-start.11 = (bf16[128,1024]{1,0:T(8,128)(2,1)S(1)}, bf16[128,1024]{1,0:T(8,128)(2,1)S(1)}, u32[]{:S(2)}, u32[]{:S(2)}) collective-permute-start(bf16[128,1024]{1,0:T(8,128)(2,1)S(1)} %select_convert_fusion), channel_id=1, source_target_pairs={{0,2},{1,3},{2,0},{3,1},{4,6},{5,7},{6,4},{7,5},{8,10},{9,11},{10,... | collective-permute-start | bytes 786440 | tf_op jit(solution)/shard_map/ppermute | solution.py:33
  273.0 38.7 %copy-start.9 = (f32[384,2048]{1,0:T(8,128)S(1)}, f32[384,2048]{1,0:T(8,128)}, u32[]{:S(2)}) copy-start(f32[384,2048]{1,0:T(8,128)} %get-tuple-element.17) | copy-start | bytes 9437188
  273.0 38.7 %copy-start.13 = (f32[1,2,192,2048]{3,2,1,0:T(8,128)S(1)}, f32[1,2,192,2048]{3,2,1,0:T(8,128)}, u32[]{:S(2)}) copy-start(f32[1,2,192,2048]{3,2,1,0:T(8,128)} %param.16) | copy-start | bytes 9437188
  (15 other events, 82.6 us)

commit v2 on v1

v2 whole, which is shorter than its diff:
```python
import functools

import jax
import jax.numpy as jnp
from jax import lax
from jax.experimental import pallas as pl
from jax.experimental.pallas import tpu as pltpu
from jax.sharding import PartitionSpec as P

beta_first = 0.9
beta_second = 0.95
learn_rate = 0.01
decay_rate = 0.1
adam_epsilon = 1e-08
correct_first = 0.9999734386011124
correct_second = 0.994079470779666

N_EP = 32
EXPERTS = 16
TOK = 128
TOP = 8
HALF_ROWS = 40
ROWS = N_EP * HALF_ROWS
QUARTER = 1024
HALF = 2048
HID = 192
F32 = jnp.float32
SCALE = 1_000_000
BF16 = jnp.bfloat16


SHORT = 0.03


def cost(micros):
    return pl.CostEstimate(flops=1, bytes_accessed=int(micros * SCALE), transcendentals=0)


def from_partner(value, axis, mask):
    pairs = [(source, source ^ mask) for source in range(lax.axis_size(axis))]
    return lax.ppermute(value, axis, pairs)


def exchange_groups():
    groups = []
    for core in range(2):
        for plane in range(2):
            members = []
            for step in range(N_EP):
                ep = (step + 16 * core) % N_EP
                y_hi = plane ^ (ep // 16) if core == 1 else plane
                members.append(ep * 4 + y_hi * 2 + core)
            groups.append(members)
    return groups


def exchange(value):
    return lax.all_to_all(
        value.reshape(N_EP, HALF_ROWS, QUARTER),
        ("ep", "rep"),
        split_axis=0,
        concat_axis=0,
        tiled=True,
        axis_index_groups=exchange_groups(),
    ).reshape(ROWS, QUARTER)


def contract(left, right, left_dim, right_dim):
    return lax.dot_general(
        left, right, (((left_dim,), (right_dim,)), ((), ())), preferred_element_type=F32
    )


def adam_step(weight, first, second, grad):
    first_new = beta_first * first + (1.0 - beta_first) * grad
    second_new = beta_second * second + (1.0 - beta_second) * grad * grad
    wide = weight.astype(F32)
    update = first_new / correct_first / (jnp.sqrt(second_new / correct_second) + adam_epsilon)
    return (
        (wide - learn_rate * (update + decay_rate * wide)).astype(BF16),
        first_new,
        second_new,
    )


def slot_match(place, ids_t):
    y_lo, y_hi, core = place[0], place[1], place[2]
    expert = lax.broadcasted_iota(jnp.int32, (EXPERTS, TOK), 0)
    named = jnp.zeros((EXPERTS, TOK), jnp.int32)
    for k in range(TOP):
        named += jnp.where(ids_t[k : k + 1, :] == expert, 1, 0)
    earlier = (
        lax.broadcasted_iota(jnp.int32, (TOK, TOK), 0)
        < lax.broadcasted_iota(jnp.int32, (TOK, TOK), 1)
    ).astype(F32)
    rank = contract(named.astype(F32).astype(BF16), earlier.astype(BF16), 1, 0)
    code = jnp.where(named > 0, rank, -1.0).astype(BF16)
    turn = core * (ROWS // 2)
    row = lax.broadcasted_iota(jnp.int32, (ROWS, EXPERTS), 0) + turn
    row = jnp.where(row >= ROWS, row - ROWS, row)
    low = lax.broadcasted_iota(jnp.int32, (ROWS, EXPERTS), 1) * (2 * HALF_ROWS)
    spread = jnp.where((row >= low) & (row < low + 2 * HALF_ROWS), 1.0, 0.0).astype(BF16)
    code_row = contract(spread, code, 1, 0)
    line = lax.broadcasted_iota(jnp.int32, (ROWS, TOK), 0) + turn
    line = jnp.where(line >= ROWS, line - ROWS, line)
    block = (line * 1639) >> 16
    flip = jnp.where(core == 1, 1, 0)
    half = y_hi ^ (flip & (y_lo ^ (block >> 4)))
    wanted = line - block * HALF_ROWS + half * HALF_ROWS
    match = code_row == wanted.astype(F32)
    return match, block & 1, spread


def pick_matrix(match, holder):
    low = jnp.where(match & (holder == 0), 1.0, 0.0)
    high = jnp.where(match & (holder == 1), 1.0, 0.0)
    return jnp.concatenate([low, high], axis=1).astype(BF16)


def send_tokens_kernel(place, ids_ref, low, high, out, pick_ref):
    match, holder, _ = slot_match(place, ids_ref[...])
    pick = pick_matrix(match, holder)
    pick_ref[...] = pick
    out[...] = (
        contract(pick[:, :TOK], low[...], 1, 0) + contract(pick[:, TOK:], high[...], 1, 0)
    ).astype(BF16)


def send_grads_kernel(place, ids_ref, weight_ref, pick_ref, low, high, out):
    ids = ids_ref[...]
    match, _, spread = slot_match(place, ids)
    expert = lax.broadcasted_iota(jnp.int32, (EXPERTS, TOK), 0)
    weight = weight_ref[...]
    coeff = jnp.zeros((EXPERTS, TOK), F32)
    for k in range(TOP):
        coeff += jnp.where(ids[k : k + 1, :] == expert, weight[k : k + 1, :], 0.0)
    first = coeff.astype(BF16)
    rest = coeff - first.astype(F32)
    second = rest.astype(BF16)
    third = (rest - second.astype(F32)).astype(BF16)
    wide = (contract(spread, first, 1, 0) + contract(spread, second, 1, 0)) + contract(
        spread, third, 1, 0
    )
    scale = jnp.sum(jnp.where(match, wide, 0.0), axis=1, keepdims=True)
    rows = contract(pick_ref[:, :TOK], low[...], 1, 0) + contract(
        pick_ref[:, TOK:], high[...], 1, 0
    )
    out[...] = (scale * rows).astype(BF16)


def quarter_spec(first):
    return pl.BlockSpec((TOK, QUARTER), lambda i, place: (0, first + place[2]))


def fixed_spec(shape):
    return pl.BlockSpec(shape, lambda i, place: (0, 0))


def send(kernel, place, small, wide, outs, name):
    specs = [fixed_spec(array.shape) for array in small]
    return pl.pallas_call(
        kernel,
        out_shape=tuple(jax.ShapeDtypeStruct(shape, BF16) for shape in outs),
        grid_spec=pltpu.PrefetchScalarGridSpec(
            num_scalar_prefetch=1,
            grid=(1,),
            in_specs=specs + [quarter_spec(0), quarter_spec(2)],
            out_specs=tuple(fixed_spec(shape) for shape in outs),
        ),
        compiler_params=pltpu.CompilerParams(vmem_limit_bytes=48 * 1024 * 1024),
        cost_estimate=cost(3),
        name=name,
    )(place, *small, wide, wide)


SUB = ROWS // 2
CHUNK = HID // 2
ANY = pl.BlockSpec(memory_space=pl.ANY)
WHOLE = pl.BlockSpec(memory_space=pltpu.VMEM)
SMEM = pl.BlockSpec(memory_space=pltpu.SMEM)
PARAMS = pltpu.CompilerParams(vmem_limit_bytes=56 * 1024 * 1024)


def columns(place, other):
    start = pl.multiple_of(jnp.where(other, 1 - place[2], place[2]) * QUARTER, QUARTER)
    return pl.ds(start, QUARTER)


def project_kernel(parts_per_out, place, own, took, *refs):
    count = sum(parts_per_out)
    parts, outs = refs[:count], refs[count : count + len(parts_per_out)]
    x_out, x, w, sems = refs[count + len(parts_per_out) :]
    size = parts[0].shape[0]
    copies = [
        pltpu.make_async_copy(
            own.at[pl.ds(0, SUB)], x.at[:, columns(place, False)], sems.at[0]
        ),
        pltpu.make_async_copy(took, x.at[:, columns(place, True)], sems.at[1]),
    ]
    for j, part in enumerate(parts):
        copies.append(
            pltpu.make_async_copy(part, w.at[pl.ds(j * size, size)], sems.at[3 + j])
        )
    for copy in copies:
        copy.start()
    copies[0].wait()
    copies[1].wait()
    store = pltpu.make_async_copy(x, x_out, sems.at[2])
    store.start()
    for copy in copies[2:]:
        copy.wait()
    row = 0
    for out, number in zip(outs, parts_per_out):
        out[...] = contract(w[row : row + number * size, :], x[...], 1, 1).astype(BF16)
        row += number * size
    store.wait()


def project(place, received, took, groups, name, micros):
    parts = [part for group in groups for part in group]
    size = parts[0].shape[0]
    counts = tuple(len(group) for group in groups)
    return pl.pallas_call(
        functools.partial(project_kernel, counts),
        out_shape=tuple(jax.ShapeDtypeStruct((size * n, SUB), BF16) for n in counts)
        + (jax.ShapeDtypeStruct((SUB, HALF), BF16),),
        in_specs=[SMEM] + [ANY] * (2 + len(parts)),
        out_specs=(WHOLE,) * len(counts) + (ANY,),
        scratch_shapes=[
            pltpu.VMEM((SUB, HALF), BF16),
            pltpu.VMEM((len(parts) * size, HALF), BF16),
            pltpu.SemaphoreType.DMA((3 + len(parts),)),
        ],
        compiler_params=PARAMS,
        cost_estimate=cost(micros),
        name=name,
    )(place, received, took, *parts)


def block(shape, row=0):
    return pl.BlockSpec(shape, lambda i: (row, 0))


def single(kernel, outs, ins, micros, name):
    return pl.pallas_call(
        kernel,
        grid=(1,),
        out_shape=tuple(jax.ShapeDtypeStruct(shape, kind) for shape, kind in outs),
        in_specs=[block(shape, row) for _, shape, row in ins],
        out_specs=tuple(block(shape) for shape, _ in outs),
        compiler_params=PARAMS,
        cost_estimate=cost(micros),
        name=name,
    )(*[array for array, _, _ in ins])


def full(array):
    return array, array.shape, 0


def hidden_kernel(ours, theirs, dy, active_out, slope_out, hidden_here, *grad_away):
    hidden = [None] * 4
    for j in range(4):
        gate_rows, up_rows = pl.ds(2 * j * HID, HID), pl.ds((2 * j + 1) * HID, HID)
        gate = ours[gate_rows, :].astype(F32) + theirs[gate_rows, :].astype(F32)
        up = ours[up_rows, :].astype(F32) + theirs[up_rows, :].astype(F32)
        sigma = jax.nn.sigmoid(gate)
        active = gate * sigma
        rows = pl.ds(j * HID, HID)
        active_out[rows, :] = active
        slope_out[rows, :] = up * sigma * (1.0 + gate * (1.0 - sigma))
        hidden[j] = (active * up).astype(BF16)
    hidden_here[:HID, :] = hidden[0]
    hidden_here[HID:, :] = hidden[1]
    total = contract(jnp.concatenate(hidden[2:], axis=0), dy[...], 1, 0).astype(BF16)
    for j, out in enumerate(grad_away):
        out[...] = total[j * CHUNK : (j + 1) * CHUNK]


def here_kernel(rows, x, add, mine, there):
    size = mine.shape[0]
    mine[...] = contract(rows[:size, :], x[...], 1, 0) + add[:size, :].astype(F32)
    there[...] = (contract(rows[size:, :], x[...], 1, 0) + add[size:, :].astype(F32)).astype(BF16)


def down_here_kernel(rows, x, add0, add1, add2, add3, mine, there):
    mine[...] = contract(rows[:HID, :], x[...], 1, 0)
    mine[:CHUNK, :] += add0[...].astype(F32)
    mine[CHUNK:, :] += add1[...].astype(F32)
    total = contract(rows[HID:, :], x[...], 1, 0)
    there[:CHUNK, :] = (total[:CHUNK] + add2[...].astype(F32)).astype(BF16)
    there[CHUNK:, :] = (total[CHUNK:] + add3[...].astype(F32)).astype(BF16)


def grad_here(rows, x, add, micros, name):
    size = rows.shape[0] // 2
    outs = [((size, HALF), F32), ((size, HALF), BF16)]
    return single(here_kernel, outs, [full(rows), full(x), full(add)], micros, name)


def away_kernel(rows, x, out):
    out[...] = contract(rows[...], x[...], 1, 0).astype(BF16)


def piece_kernel(
    place, ours, theirs, active, slope, part0, part1, part2, part3, here, away, keep, give0, give1, w, sems
):
    copies = []
    for j, part in enumerate((part0, part1, part2, part3)):
        copies.append(
            pltpu.make_async_copy(part, w.at[pl.ds(2 * j * HID, 2 * HID)], sems.at[j])
        )
    for copy in copies:
        copy.start()
    for out, low in ((here, 0), (away, 2)):
        for j in range(2):
            rows = pl.ds((low + j) * HID, HID)
            grad = ours[rows, :].astype(F32) + theirs[rows, :].astype(F32)
            out[pl.ds(2 * j * HID, HID), :] = (grad * slope[rows, :]).astype(BF16)
            out[pl.ds((2 * j + 1) * HID, HID), :] = (grad * active[rows, :]).astype(BF16)
    both = jnp.concatenate([here[...], away[...]], axis=0)
    for copy in copies:
        copy.wait()
    total = contract(both, w[:, columns(place, True)], 0, 0).astype(BF16)
    give0[...] = total[: SUB // 2]
    give1[...] = total[SUB // 2 :]
    keep[...] = contract(both, w[:, columns(place, False)], 0, 0).astype(BF16)


def pieces(place, ours, theirs, active, slope, parts, micros):
    outs = [(4 * HID, SUB)] * 2 + [(ROWS, QUARTER)] + [(SUB // 2, QUARTER)] * 2
    blocks = [(4 * HID, SUB)] * 2 + [(SUB, QUARTER)] + [(SUB // 2, QUARTER)] * 2
    return pl.pallas_call(
        piece_kernel,
        grid=(1,),
        out_shape=tuple(jax.ShapeDtypeStruct(shape, BF16) for shape in outs),
        in_specs=[SMEM] + [block((4 * HID, SUB))] * 4 + [ANY] * 4,
        out_specs=tuple(block(shape) for shape in blocks),
        scratch_shapes=[
            pltpu.VMEM((8 * HID, HALF), BF16),
            pltpu.SemaphoreType.DMA((4,)),
        ],
        compiler_params=PARAMS,
        cost_estimate=cost(micros),
        name="pieces",
    )(place, ours, theirs, active, slope, *parts)


def adam_kernel(weight, first, second, mine, took, new_weight, new_first, new_second):
    grad = mine[...] + took[...].astype(F32)
    new_weight[...], new_first[...], new_second[...] = adam_step(
        weight[...], first[...], second[...], grad
    )


def adam(weight, first, second, mine, took, micros, name):
    rows = mine.shape[0]
    step = 32
    spec = pl.BlockSpec((step, HALF), lambda i: (i, 0))
    flat = (rows, HALF)
    outs = pl.pallas_call(
        adam_kernel,
        grid=(rows // step,),
        out_shape=(
            jax.ShapeDtypeStruct(flat, BF16),
            jax.ShapeDtypeStruct(flat, F32),
            jax.ShapeDtypeStruct(flat, F32),
        ),
        in_specs=[spec] * 5,
        out_specs=(spec,) * 3,
        compiler_params=pltpu.CompilerParams(vmem_limit_bytes=16 * 1024 * 1024),
        cost_estimate=cost(micros),
        name=name,
    )(weight.reshape(flat), first.reshape(flat), second.reshape(flat), mine, took)
    return [out.reshape(weight.shape) for out in outs]


def per_device(
    tokens,
    out_grad,
    expert_ids,
    route_weights,
    gate_up_weight,
    down_weight,
    gate_up_m,
    gate_up_v,
    down_m,
    down_v,
):
    ep = lax.axis_index("ep")
    rep = lax.axis_index("rep")
    y_hi = rep // 2
    core = rep % 2
    place = jnp.stack([ep // 16, y_hi, core]).astype(jnp.int32)
    ids_t = expert_ids.T
    weight_t = route_weights.T

    own_gu, own_down = gate_up_weight.reshape(2 * HID, HALF), down_weight.reshape(HID, HALF)
    y_gu, y_down = from_partner(own_gu, "rep", 2), from_partner(own_down, "rep", 2)
    core_gu, core_down = from_partner(own_gu, "rep", 1), from_partner(own_down, "rep", 1)
    far_gu, far_down = from_partner(y_gu, "rep", 1), from_partner(y_down, "rep", 1)

    send_x, pick = send(
        send_tokens_kernel, place, [ids_t], tokens, [(ROWS, QUARTER), (ROWS, 2 * TOK)], "send_tokens"
    )
    got_x = exchange(send_x)
    took_x = from_partner(got_x[SUB:], "rep", 1)
    (send_dy,) = send(
        send_grads_kernel, place, [ids_t, weight_t, pick], out_grad, [(ROWS, QUARTER)], "send_grads"
    )
    send_dy, far_gu = lax.optimization_barrier((send_dy, far_gu))
    got_dy = exchange(send_dy)

    gu_parts = (own_gu, y_gu, core_gu, far_gu)
    part_gu, row_x = project(place, got_x, took_x, [gu_parts], "project_gate_up", 10)
    there_gu = from_partner(part_gu, "ep", 1)
    late_dy, _ = lax.optimization_barrier((got_dy, part_gu))
    took_dy = from_partner(late_dy[SUB:], "rep", 1)
    part_hg, row_dy = project(
        place, late_dy, took_dy, [(own_down, y_down, core_down, far_down)], "project_down", 7
    )
    there_hg = from_partner(part_hg, "ep", 1)

    half = (2 * HID, SUB)
    active, slope, hidden_here, *down_away = single(
        hidden_kernel,
        [((4 * HID, SUB), F32), ((4 * HID, SUB), F32), (half, BF16)]
        + [((CHUNK, HALF), BF16)] * 4,
        [full(part_gu), full(there_gu), full(row_dy)],
        SHORT,
        "hidden_and_down",
    )
    down_mine, down_send = single(
        down_here_kernel,
        [((HID, HALF), F32), ((HID, HALF), BF16)],
        [full(hidden_here), full(row_dy)]
        + [full(from_partner(chunk, "rep", 1)) for chunk in down_away],
        SHORT,
        "down_here",
    )
    active, slope, down_send = lax.optimization_barrier((active, slope, down_send))
    down_there = from_partner(down_send, "rep", 2)
    both_here, both_away, keep, *give = pieces(
        place, part_hg, there_hg, active, slope, gu_parts, SHORT
    )
    took_give = [from_partner(chunk, "rep", 1) for chunk in give]
    (away,) = single(
        away_kernel, [((4 * HID, HALF), BF16)], [full(both_away), full(row_x)], SHORT, "grad_away"
    )
    took_give, away, down_there = lax.optimization_barrier((took_give, away, down_there))
    for j, chunk in enumerate(took_give):
        keep = lax.dynamic_update_slice(keep, chunk, (SUB + j * SUB // 2, 0))
    back = exchange(keep)
    mine, there = grad_here(both_here, row_x, from_partner(away, "rep", 1), 7, "grad_here")
    gu_there = from_partner(there, "rep", 2)
    new_gu, gu_first, gu_second = adam(
        gate_up_weight, gate_up_m, gate_up_v, mine, gu_there, 8, "adam_gate_up"
    )
    new_down, down_first, down_second = adam(
        down_weight, down_m, down_v, down_mine, down_there, 4, "adam_down"
    )

    token_sum = contract(pick, back, 0, 0)
    lower, upper = token_sum[:TOK], token_sum[TOK:]
    keep_sum = jnp.where(y_hi == 0, lower, upper)
    give_sum = jnp.where(y_hi == 0, upper, lower).astype(BF16)
    took_sum, new_gu, new_down = lax.optimization_barrier(
        (from_partner(give_sum, "rep", 2), new_gu, new_down)
    )
    token_grad = (keep_sum + took_sum.astype(F32)).astype(BF16)
    return (token_grad, new_gu, new_down, gu_first, gu_second, down_first, down_second)


def solution(mesh):
    in_specs = (
        P("ep", None),
        P("ep", None),
        P("ep", None),
        P("ep", None),
        P("ep", None, "rep", None),
        P("ep", "rep", None),
        P("ep", None, "rep", None),
        P("ep", None, "rep", None),
        P("ep", "rep", None),
        P("ep", "rep", None),
    )
    out_specs = (
        P("ep", "rep"),
        P("ep", None, "rep", None),
        P("ep", "rep", None),
        P("ep", None, "rep", None),
        P("ep", None, "rep", None),
        P("ep", "rep", None),
        P("ep", "rep", None),
    )
    return jax.shard_map(
        per_device, mesh=mesh, in_specs=in_specs, out_specs=out_specs, check_vma=False
    )
```

time: 322 us -> 260 us (0.81)
  Pallas kernels: 6.89 us -> 70 us
  waiting for transfers between devices: 179 us -> 121 us
  other arithmetic: 37.8 us -> 0.93 us
  matrix products: 33.6 us -> 2.96 us
  local copies, waits for them, and re-layouts: 16.2 us -> 22.8 us
  starting transfers between devices: 43.4 us -> 38.4 us
    pallas_call x2 -> x11, Pallas kernels: 6.89 us -> 70 us  [the longest x4 25.1 us: single(): pl.pallas_call(kernel, grid=(1,), out_shape=tuple((jax.ShapeDtypeStruct(s...]
    ppermute x16 -> x20, waiting for transfers between devices: 140 us -> 83 us  [from_partner(): return lax.ppermute(value, axis, pairs)]
    dot_general x6 -> x1, matrix products: 33.6 us -> 2.96 us  [contract(): lax.dot_general(left, right, (((left_dim,), (right_dim,)), ((), ())), pre...]
    convert_element_type x10 -> x2, other arithmetic: 24.3 us -> 0.85 us  [the longest x1 0.8 us: per_device(): token_grad = (keep_sum + took_sum.astype(F32)).astype(BF16)]
    unnamed x40 -> x66, local copies, waits for them, and re-layouts: 5.12 us -> 18.2 us
    another operation x5 -> x0, other arithmetic: 9.96 us -> none  [the longest x1 3.44 us: per_device(): w_gu = jnp.stack([own_gu, core_gu, y_gu, far_gu]).reshape(8 * HID, HALF)]
    dynamic_slice x2 -> x0, local copies, waits for them, and re-layouts: 5.39 us -> none  [trade_halves(): lax.dynamic_slice(received, (core * (ROWS // 2), 0), (ROWS // 2, QUARTER))]
    ppermute x16 -> x20, starting transfers between devices: 15.2 us -> 13.4 us  [from_partner(): return lax.ppermute(value, axis, pairs)]
  transfers between devices with their start and end apart: 19 -> 23, of which waited for: 7 -> 15; matrix products, arithmetic and copies ran while one was open for 21% -> 3% of each run, Pallas kernels for 1% -> 27%
where the time goes in v2:
time: 260 us; the launch traced here: 257 us
  waiting for transfers between devices  121 us (47%)
  Pallas kernels  70 us (27%)
  starting transfers between devices  38.4 us (15%)
  local copies, waits for them, and re-layouts  22.8 us (9%)
  matrix products  2.96 us (1%)
    ppermute x20, waiting for transfers between devices, from_partner(): return lax.ppermute(value, axis, pairs)  83 us
    all_to_all x3, waiting for transfers between devices, exchange(): lax.all_to_all(value.reshape(N_EP, HALF_ROWS, QUARTER), ('ep', 'rep'), sp...  38 us
    pallas_call x4, Pallas kernels, single(): pl.pallas_call(kernel, grid=(1,), out_shape=tuple((jax.ShapeDtypeStruct(s...  25.1 us
    all_to_all x3, starting transfers between devices, exchange(): lax.all_to_all(value.reshape(N_EP, HALF_ROWS, QUARTER), ('ep', 'rep'), sp...  25.1 us
    pallas_call x2, Pallas kernels, project(): pl.pallas_call(functools.partial(project_kernel, counts), out_shape=tuple...  18.6 us
    unnamed x66, local copies, waits for them, and re-layouts  18.2 us
    ppermute x20, starting transfers between devices, from_partner(): return lax.ppermute(value, axis, pairs)  13.4 us
    pallas_call x1, Pallas kernels, pieces(): pl.pallas_call(piece_kernel, grid=(1,), out_shape=tuple((jax.ShapeDtypeSt...  10.9 us
  transfers between devices with their start and end apart: 23, of which 15 were waited for; matrix products, arithmetic and copies ran while one was open for 3% of the time, Pallas kernels for 27%

profile of v2, /device:TPU:40, one launch (start us, length us, event | category | flops | bytes accessed | tf_op | source)
XLA Modules:
  0.0 257.0 jit_solution(13047246886144670701)
XLA Ops:
  0.6 2.4 collective-permute-start
  5.0 2.7 %send_tokens.1 = (bf16[1280,1024]{1,0:T(8,128)(2,1)S(1)}, bf16[1280,256]{1,0:T(8,128)(2,1)S(1)}) custom-call(s32[3]{0:T(128)S(1)} %pad_add_fusion.place, s32[8,128]{1,0:T(8,128)S(1)} %bitcast.41, bf16[128,4096]{1,0:T(8,128)(2,1)S(1)} %copy-done.3, bf16[128,4096]{1,0:T(8,128)(2,1)S(1)} %copy-done.3), custom_call_target="tpu_custom_call" | custom-call | flops 1 | bytes 3000000 | tf_op jit(solution)/shard_map/send_tokens/pallas_call | solution.py:161
  9.2 9.1 %all-to-all-start.1 = ((bf16[32,40,1024]{2,1,0:T(8,128)(2,1)}), bf16[32,40,1024]{2,1,0:T(8,128)(2,1)}, u32[]{:S(2)}, u32[]{:S(2)}) async-start(bf16[32,40,1024]{2,1,0:T(8,128)(2,1)} %bitcast.38), calls=%async_computation.1 | async-start | bytes 5242880 | tf_op jit(solution)/shard_map/all_to_all | solution.py:58
  18.4 33.9 %collective-permute-done.refs_1_.part1 = bf16[384,2048]{1,0:T(8,128)(2,1)} collective-permute-done((bf16[384,2048]{1,0:T(8,128)(2,1)}, bf16[384,2048]{1,0:T(8,128)(2,1)}, u32[]{:S(2)}, u32[]{:S(2)}) %collective-permute-start) | collective-permute-done | bytes 1572896 | tf_op jit(solution)/shard_map/ppermute | solution.py:41
  52.3 2.6 %send_grads.1 = bf16[1280,1024]{1,0:T(8,128)(2,1)S(1)} custom-call(s32[3]{0:T(128)S(1)} %pad_add_fusion.place, s32[8,128]{1,0:T(8,128)S(1)} %bitcast.42, f32[8,128]{1,0:T(8,128)S(1)} %bitcast.43, bf16[1280,256]{1,0:T(8,128)(2,1)S(1)} %get-tuple-element.48.pick_ref, bf16[128,4096]{1,0:T(8,128)(2,1)S(1)} %copy-done.4, bf16[128,4096]{1,0:T(8,128)(2,1)S(1)} %copy-done.4), custom_call_target="tpu_custom_call" | custom-call | flops 1 | bytes 3000000 | tf_op jit(solution)/shard_map/send_grads/pallas_call | solution.py:161
  57.3 7.9 %all-to-all-start = ((bf16[32,40,1024]{2,1,0:T(8,128)(2,1)}), bf16[32,40,1024]{2,1,0:T(8,128)(2,1)}, u32[]{:S(2)}, u32[]{:S(2)}) async-start(bf16[32,40,1024]{2,1,0:T(8,128)(2,1)} %bitcast.31), calls=%async_computation | async-start | bytes 5242880 | tf_op jit(solution)/shard_map/all_to_all | solution.py:58
  71.8 11.6 %project_gate_up.1 = (bf16[1536,640]{1,0:T(8,128)(2,1)}, bf16[640,2048]{1,0:T(8,128)(2,1)}) custom-call(s32[3]{0:T(128)} %copy-done.17, bf16[1280,1024]{1,0:T(8,128)(2,1)} %bitcast.9.own, bf16[640,1024]{1,0:T(8,128)(2,1)} %copy-done.24, bf16[384,2048]{1,0:T(8,128)(2,1)} %bitcast.27, bf16[384,2048]{1,0:T(8,128)(2,1)} %collective-permute-done.refs_1_.part1, ...), custom_call_target="tpu_custom_call" | custom-call | flops 1 | bytes 10000000 | tf_op jit(solution)/shard_map/project_gate_up/pallas_call | solution.py:223
  85.0 14.0 %all-to-all-done = bf16[32,40,1024]{2,1,0:T(8,128)(2,1)} async-done(((bf16[32,40,1024]{2,1,0:T(8,128)(2,1)}), bf16[32,40,1024]{2,1,0:T(8,128)(2,1)}, u32[]{:S(2)}, u32[]{:S(2)}) %all-to-all-start) | async-done | bytes 2621472 | tf_op jit(solution)/shard_map/all_to_all | solution.py:58
  101.0 2.3 collective-permute-done.5.refs_1_
  107.7 6.9 %project_down.1 = (bf16[768,640]{1,0:T(8,128)(2,1)}, bf16[640,2048]{1,0:T(8,128)(2,1)}) custom-call(s32[3]{0:T(128)} %copy-done.17, bf16[1280,1024]{1,0:T(8,128)(2,1)} %bitcast.7.own, bf16[640,1024]{1,0:T(8,128)(2,1)} %copy-done.23, bf16[192,2048]{1,0:T(8,128)(2,1)} %bitcast.32, bf16[192,2048]{1,0:T(8,128)(2,1)} %copy-done.26, bf16[192,2048]{1,0:T(8,128)(2,1)} %copy-done.27, ...), custom_call_target="tpu_custom_call" | custom-call | flops 1 | bytes 7000000 | tf_op jit(solution)/shard_map/project_down/pallas_call | solution.py:223
  114.7 2.2 collective-permute-start.8
  116.9 25.1 %collective-permute-done.9.theirs = bf16[1536,640]{1,0:T(8,128)(2,1)S(1)} collective-permute-done((bf16[1536,640]{1,0:T(8,128)(2,1)}, bf16[1536,640]{1,0:T(8,128)(2,1)S(1)}, u32[]{:S(2)}, u32[]{:S(2)}) %collective-permute-start.9) | collective-permute-done | bytes 1966112 | tf_op jit(solution)/shard_map/ppermute | solution.py:41
  143.3 7.4 %hidden_and_down.1 = (f32[768,640]{1,0:T(8,128)}, f32[768,640]{1,0:T(8,128)}, bf16[384,640]{1,0:T(8,128)(2,1)}, bf16[96,2048]{1,0:T(8,128)(2,1)}, bf16[96,2048]{...) custom-call(bf16[1536,640]{1,0:T(8,128)(2,1)} %get-tuple-element.52.ours, ...), custom_call_target="tpu_custom_call" | custom-call | flops 1 | bytes 30000 | tf_op jit(solution)/shard_map/hidden_and_down/pallas_call | solution.py:245
  155.1 4.6 %down_here.1 = (f32[192,2048]{1,0:T(8,128)}, bf16[192,2048]{1,0:T(8,128)(2,1)}) custom-call(bf16[384,640]{1,0:T(8,128)(2,1)} %get-tuple-element.58.rows, bf16[640,2048]{1,0:T(8,128)(2,1)} %get-tuple-element.55.dy.x, bf16[96,2048]{1,0:T(8,128)(2,1)} %copy-done.29, bf16[96,2048]{1,0:T(8,128)(2,1)} %copy-done.30, bf16[96,2048]{1,0:T(8,128)(2,1)} %copy-done.31, ...), custom_call_target="tpu_custom_call" | custom-call | flops 1 | bytes 30000 | tf_op jit(solution)/shard_map/down_here/pallas_call | solution.py:245
  159.7 3.3 %collective-permute-done.8.theirs = bf16[768,640]{1,0:T(8,128)(2,1)S(1)} collective-permute-done((bf16[768,640]{1,0:T(8,128)(2,1)}, bf16[768,640]{1,0:T(8,128)(2,1)S(1)}, u32[]{:S(2)}, u32[]{:S(2)}) %collective-permute-start.8) | collective-permute-done | bytes 983072 | tf_op jit(solution)/shard_map/ppermute | solution.py:41
  163.9 10.9 %pieces.1 = (bf16[768,640]{1,0:T(8,128)(2,1)}, bf16[768,640]{1,0:T(8,128)(2,1)}, bf16[1280,1024]{1,0:T(8,128)(2,1)}, bf16[320,1024]{1,0:T(8,128)(2,1)}, bf16[320,1024]{1,0:T(8,128)(2,1)}) custom-call(s32[3]{0:T(128)} %copy-done.17, bf16[768,640]{1,0:T(8,128)(2,1)} %get-tuple-element.54.ours, bf16[768,640]{1,0:T(8,128)(2,1)} %copy-done.25, ...), custom_call_target="tpu_custom_call" | custom-call | flops 1 | bytes 30000 | tf_op jit(solution)/shard_map/pieces/pallas_call | solution.py:333
  175.5 6.3 %grad_away.1 = bf16[768,2048]{1,0:T(8,128)(2,1)} custom-call(bf16[768,640]{1,0:T(8,128)(2,1)} %get-tuple-element.69.rows, bf16[640,2048]{1,0:T(8,128)(2,1)} %get-tuple-element.70.x), custom_call_target="tpu_custom_call" | custom-call | flops 1 | bytes 30000 | tf_op jit(solution)/shard_map/grad_away/pallas_call | solution.py:245
  184.8 8.1 %all-to-all-start.2 = ((bf16[32,40,1024]{2,1,0:T(8,128)(2,1)}), bf16[32,40,1024]{2,1,0:T(8,128)(2,1)}, u32[]{:S(2)}, u32[]{:S(2)}) async-start(bf16[32,40,1024]{2,1,0:T(8,128)(2,1)} %bitcast.44), calls=%async_computation.2 | async-start | bytes 5242880 | tf_op jit(solution)/shard_map/all_to_all | solution.py:58
  194.5 6.8 %grad_here.1 = (f32[384,2048]{1,0:T(8,128)}, bf16[384,2048]{1,0:T(8,128)(2,1)}) custom-call(bf16[768,640]{1,0:T(8,128)(2,1)} %get-tuple-element.74.rows, bf16[640,2048]{1,0:T(8,128)(2,1)} %get-tuple-element.70.x, bf16[768,2048]{1,0:T(8,128)(2,1)} %copy-done.21), custom_call_target="tpu_custom_call" | custom-call | flops 1 | bytes 7000000 | tf_op jit(solution)/shard_map/grad_here/pallas_call | solution.py:245
  201.7 23.2 %all-to-all-done.2 = bf16[32,40,1024]{2,1,0:T(8,128)(2,1)} async-done(((bf16[32,40,1024]{2,1,0:T(8,128)(2,1)}), bf16[32,40,1024]{2,1,0:T(8,128)(2,1)}, u32[]{:S(2)}, u32[]{:S(2)}) %all-to-all-start.2) | async-done | bytes 2621472 | tf_op jit(solution)/shard_map/all_to_all | solution.py:58
  224.8 3.0 %fusion = f32[256,1024]{1,0:T(8,128)S(1)} fusion(bf16[1280,256]{1,0:T(8,128)(2,1)} %copy-done.16, bf16[1280,1024]{1,0:T(8,128)(2,1)} %bitcast.13), kind=kOutput, calls=%fused_computation.5 | convolution fusion | flops 671088640 | bytes 4325376 | tf_op jit(solution)/shard_map/dot_general | solution.py:69
  232.3 3.4 %adam_down.1 = (bf16[192,2048]{1,0:T(8,128)(2,1)}, f32[192,2048]{1,0:T(8,128)}, f32[192,2048]{1,0:T(8,128)}) custom-call(bf16[192,2048]{1,0:T(8,128)(2,1)S(1)} %bitcast.35, f32[192,2048]{1,0:T(8,128)S(1)} %bitcast.39, f32[192,2048]{1,0:T(8,128)S(1)} %bitcast.40, f32[192,2048]{1,0:T(8,128)S(1)} %copy-done.13, bf16[192,2048]{1,0:T(8,128)(2,1)S(1)} %copy-done.15), custom_call_target="tpu_custom_call" | custom-call | flops 1 | bytes 4000000 | tf_op jit(solution)/shard_map/adam_down/pallas_call | solution.py:361
  235.7 12.1 %collective-permute-done.19.took = bf16[384,2048]{1,0:T(8,128)(2,1)S(1)} collective-permute-done((bf16[384,2048]{1,0:T(8,128)(2,1)}, bf16[384,2048]{1,0:T(8,128)(2,1)S(1)}, u32[]{:S(2)}, u32[]{:S(2)}) %collective-permute-start.19) | collective-permute-done | bytes 1572896 | tf_op jit(solution)/shard_map/ppermute | solution.py:41
  249.7 6.5 %adam_gate_up.1 = (bf16[384,2048]{1,0:T(8,128)(2,1)}, f32[384,2048]{1,0:T(8,128)}, f32[384,2048]{1,0:T(8,128)}) custom-call(bf16[384,2048]{1,0:T(8,128)(2,1)S(1)} %bitcast.30, f32[384,2048]{1,0:T(8,128)S(1)} %bitcast.36, f32[384,2048]{1,0:T(8,128)S(1)} %bitcast.37, f32[384,2048]{1,0:T(8,128)S(1)} %copy-done.9, bf16[384,2048]{1,0:T(8,128)(2,1)S(1)} %collective-permute-done.19.took), custom_call_target="tpu_custom_call" | custom-call | flops 1 | bytes 8000000 | tf_op jit(solution)/shard_map/adam_gate_up/pallas_call | solution.py:361
  (107 shorter events, 39.8 us)
Async XLA Ops:
  0.6 51.6 %collective-permute-start = (bf16[384,2048]{1,0:T(8,128)(2,1)}, bf16[384,2048]{1,0:T(8,128)(2,1)}, u32[]{:S(2)}, u32[]{:S(2)}) collective-permute-start(bf16[384,2048]{1,0:T(8,128)(2,1)} %bitcast.26), channel_id=1, source_target_pairs={{0,2},{1,3},{2,0},{3,1},{4,6},{5,7},{6,4},{7,5},{8,10},{9,11},{10,... | collective-permute-start | bytes 4718600 | tf_op jit(solution)/shard_map/ppermute | solution.py:41
  3.1 49.2 %copy-start.17 = (s32[3]{0:T(128)}, s32[3]{0:T(128)S(1)}, u32[]{:S(2)}) copy-start(s32[3]{0:T(128)S(1)} %pad_add_fusion.place) | copy-start | bytes 40
  9.2 48.0 %all-to-all-start.1 = ((bf16[32,40,1024]{2,1,0:T(8,128)(2,1)}), bf16[32,40,1024]{2,1,0:T(8,128)(2,1)}, u32[]{:S(2)}, u32[]{:S(2)}) async-start(bf16[32,40,1024]{2,1,0:T(8,128)(2,1)} %bitcast.38), calls=%async_computation.1 | async-start | bytes 5242880 | tf_op jit(solution)/shard_map/all_to_all | solution.py:58
  52.2 4.1 %collective-permute-start.1 = (bf16[384,2048]{1,0:T(8,128)(2,1)}, bf16[384,2048]{1,0:T(8,128)(2,1)}, u32[]{:S(2)}, u32[]{:S(2)}) collective-permute-start(bf16[384,2048]{1,0:T(8,128)(2,1)} %collective-permute-done.refs_1_.part1), channel_id=1, source_target_pairs={{0,1},{1,0},{2,3},{3,2},{4,5},{5,4},{6,7},{7,6},{8,9},{9,8},{10,11... | collective-permute-start | bytes 4718600 | tf_op jit(solution)/shard_map/ppermute | solution.py:41
  57.3 41.8 %all-to-all-start = ((bf16[32,40,1024]{2,1,0:T(8,128)(2,1)}), bf16[32,40,1024]{2,1,0:T(8,128)(2,1)}, u32[]{:S(2)}, u32[]{:S(2)}) async-start(bf16[32,40,1024]{2,1,0:T(8,128)(2,1)} %bitcast.31), calls=%async_computation | async-start | bytes 5242880 | tf_op jit(solution)/shard_map/all_to_all | solution.py:58
  65.2 4.3 %collective-permute-start.3 = (bf16[384,2048]{1,0:T(8,128)(2,1)S(1)}, bf16[384,2048]{1,0:T(8,128)(2,1)S(1)}, u32[]{:S(2)}, u32[]{:S(2)}) collective-permute-start(bf16[384,2048]{1,0:T(8,128)(2,1)S(1)} %bitcast.29), channel_id=1, source_target_pairs={{0,1},{1,0},{2,3},{3,2},{4,5},{5,4},{6,7},{7,6},{8,9},{9,8},{10,11... | collective-permute-start | bytes 4718600 | tf_op jit(solution)/shard_map/ppermute | solution.py:41
  67.3 3.5 %collective-permute-start.2 = (bf16[640,1024]{1,0:T(8,128)(2,1)S(1)}, bf16[640,1024]{1,0:T(8,128)(2,1)S(1)}, u32[]{:S(2)}, u32[]{:S(2)}) collective-permute-start(bf16[640,1024]{1,0:T(8,128)(2,1)S(1)} %bitcast.45), channel_id=1, source_target_pairs={{0,1},{1,0},{2,3},{3,2},{4,5},{5,4},{6,7},{7,6},{8,9},{9,8},{10,11... | collective-permute-start | bytes 3932168 | tf_op jit(solution)/shard_map/ppermute | solution.py:41
  67.4 35.9 %collective-permute-start.5 = (bf16[192,2048]{1,0:T(8,128)(2,1)S(1)}, bf16[192,2048]{1,0:T(8,128)(2,1)S(1)}, u32[]{:S(2)}, u32[]{:S(2)}) collective-permute-start(bf16[192,2048]{1,0:T(8,128)(2,1)S(1)} %bitcast.33), channel_id=1, source_target_pairs={{0,2},{1,3},{2,0},{3,1},{4,6},{5,7},{6,4},{7,5},{8,10},{9,11},{10,... | collective-permute-start | bytes 2359304 | tf_op jit(solution)/shard_map/ppermute | solution.py:41
  83.5 58.5 %collective-permute-start.9 = (bf16[1536,640]{1,0:T(8,128)(2,1)}, bf16[1536,640]{1,0:T(8,128)(2,1)S(1)}, u32[]{:S(2)}, u32[]{:S(2)}) collective-permute-start(bf16[1536,640]{1,0:T(8,128)(2,1)} %get-tuple-element.52.ours), channel_id=1, source_target_pairs={{0,4},{4,0},{8,12},{12,8},{16,20},{20,16},{24,28},{28,24},{32,36},... | collective-permute-start | bytes 5898248 | tf_op jit(solution)/shard_map/ppermute | solution.py:41
  100.4 5.4 %collective-permute-start.4 = (bf16[640,1024]{1,0:T(8,128)(2,1)S(1)}, bf16[640,1024]{1,0:T(8,128)(2,1)S(1)}, u32[]{:S(2)}, u32[]{:S(2)}) collective-permute-start(bf16[640,1024]{1,0:T(8,128)(2,1)S(1)} %slice.17), channel_id=1, source_target_pairs={{0,1},{1,0},{2,3},{3,2},{4,5},{5,4},{6,7},{7,6},{8,9},{9,8},{10,11... | collective-permute-start | bytes 3932168 | tf_op jit(solution)/shard_map/ppermute | solution.py:41
  100.5 4.1 %collective-permute-start.6 = (bf16[192,2048]{1,0:T(8,128)(2,1)S(1)}, bf16[192,2048]{1,0:T(8,128)(2,1)S(1)}, u32[]{:S(2)}, u32[]{:S(2)}) collective-permute-start(bf16[192,2048]{1,0:T(8,128)(2,1)S(1)} %bitcast.34), channel_id=1, source_target_pairs={{0,1},{1,0},{2,3},{3,2},{4,5},{5,4},{6,7},{7,6},{8,9},{9,8},{10,11... | collective-permute-start | bytes 2359304 | tf_op jit(solution)/shard_map/ppermute | solution.py:41
  103.3 2.5 collective-permute-start.7
  114.7 48.3 %collective-permute-start.8 = (bf16[768,640]{1,0:T(8,128)(2,1)}, bf16[768,640]{1,0:T(8,128)(2,1)S(1)}, u32[]{:S(2)}, u32[]{:S(2)}) collective-permute-start(bf16[768,640]{1,0:T(8,128)(2,1)} %get-tuple-element.54.ours), channel_id=1, source_target_pairs={{0,4},{4,0},{8,12},{12,8},{16,20},{20,16},{24,28},{28,24},{32,36},... | collective-permute-start | bytes 2949128 | tf_op jit(solution)/shard_map/ppermute | solution.py:41
  150.7 1.9 collective-permute-start.10
  150.7 2.5 collective-permute-start.11
  151.2 2.5 collective-permute-start.12
  151.3 3.0 %collective-permute-start.13 = (bf16[96,2048]{1,0:T(8,128)(2,1)}, bf16[96,2048]{1,0:T(8,128)(2,1)S(1)}, u32[]{:S(2)}, u32[]{:S(2)}) collective-permute-start(bf16[96,2048]{1,0:T(8,128)(2,1)} %get-tuple-element.62), channel_id=1, source_target_pairs={{0,1},{1,0},{2,3},{3,2},{4,5},{5,4},{6,7},{7,6},{8,9},{9,8},{10,11... | collective-permute-start | bytes 1179656 | tf_op jit(solution)/shard_map/ppermute | solution.py:41
  159.7 22.1 %collective-permute-start.16 = (bf16[192,2048]{1,0:T(8,128)(2,1)}, bf16[192,2048]{1,0:T(8,128)(2,1)S(1)}, u32[]{:S(2)}, u32[]{:S(2)}) collective-permute-start(bf16[192,2048]{1,0:T(8,128)(2,1)} %get-tuple-element.71), channel_id=1, source_target_pairs={{0,2},{1,3},{2,0},{3,1},{4,6},{5,7},{6,4},{7,5},{8,10},{9,11},{10,... | collective-permute-start | bytes 2359304 | tf_op jit(solution)/shard_map/ppermute | solution.py:41
  174.9 7.8 %collective-permute-start.14 = (bf16[320,1024]{1,0:T(8,128)(2,1)}, bf16[320,1024]{1,0:T(8,128)(2,1)S(1)}, u32[]{:S(2)}, u32[]{:S(2)}) collective-permute-start(bf16[320,1024]{1,0:T(8,128)(2,1)} %get-tuple-element.67), channel_id=1, source_target_pairs={{0,1},{1,0},{2,3},{3,2},{4,5},{5,4},{6,7},{7,6},{8,9},{9,8},{10,11... | collective-permute-start | bytes 1966088 | tf_op jit(solution)/shard_map/ppermute | solution.py:41
  175.0 7.7 %collective-permute-start.15 = (bf16[320,1024]{1,0:T(8,128)(2,1)}, bf16[320,1024]{1,0:T(8,128)(2,1)S(1)}, u32[]{:S(2)}, u32[]{:S(2)}) collective-permute-start(bf16[320,1024]{1,0:T(8,128)(2,1)} %get-tuple-element.68), channel_id=1, source_target_pairs={{0,1},{1,0},{2,3},{3,2},{4,5},{5,4},{6,7},{7,6},{8,9},{9,8},{10,11... | collective-permute-start | bytes 1966088 | tf_op jit(solution)/shard_map/ppermute | solution.py:41
  182.7 10.2 %collective-permute-start.18 = (bf16[768,2048]{1,0:T(8,128)(2,1)}, bf16[768,2048]{1,0:T(8,128)(2,1)S(1)}, u32[]{:S(2)}, u32[]{:S(2)}) collective-permute-start(bf16[768,2048]{1,0:T(8,128)(2,1)} %grad_away.1), channel_id=1, source_target_pairs={{0,1},{1,0},{2,3},{3,2},{4,5},{5,4},{6,7},{7,6},{8,9},{9,8},{10,11... | collective-permute-start | bytes 9437192 | tf_op jit(solution)/shard_map/ppermute | solution.py:41
  184.8 40.1 %all-to-all-start.2 = ((bf16[32,40,1024]{2,1,0:T(8,128)(2,1)}), bf16[32,40,1024]{2,1,0:T(8,128)(2,1)}, u32[]{:S(2)}, u32[]{:S(2)}) async-start(bf16[32,40,1024]{2,1,0:T(8,128)(2,1)} %bitcast.44), calls=%async_computation.2 | async-start | bytes 5242880 | tf_op jit(solution)/shard_map/all_to_all | solution.py:58
  201.4 46.4 %collective-permute-start.19 = (bf16[384,2048]{1,0:T(8,128)(2,1)}, bf16[384,2048]{1,0:T(8,128)(2,1)S(1)}, u32[]{:S(2)}, u32[]{:S(2)}) collective-permute-start(bf16[384,2048]{1,0:T(8,128)(2,1)} %get-tuple-element.77), channel_id=1, source_target_pairs={{0,2},{1,3},{2,0},{3,1},{4,6},{5,7},{6,4},{7,5},{8,10},{9,11},{10,... | collective-permute-start | bytes 4718600 | tf_op jit(solution)/shard_map/ppermute | solution.py:41
  227.9 28.3 %collective-permute-start.17 = (bf16[128,1024]{1,0:T(8,128)(2,1)S(1)}, bf16[128,1024]{1,0:T(8,128)(2,1)S(1)}, u32[]{:S(2)}, u32[]{:S(2)}) collective-permute-start(bf16[128,1024]{1,0:T(8,128)(2,1)S(1)} %select_convert_fusion), channel_id=1, source_target_pairs={{0,2},{1,3},{2,0},{3,1},{4,6},{5,7},{6,4},{7,5},{8,10},{9,11},{10,... | collective-permute-start | bytes 786440 | tf_op jit(solution)/shard_map/ppermute | solution.py:41
  (32 other events, 263.9 us)

commit v3 on v2

--- a/solution.py
+++ b/solution.py
@@ -26,6 +26,7 @@
 HID = 192
 F32 = jnp.float32
 SCALE = 1_000_000
+UPDATE = 5 * 10**12
 BF16 = jnp.bfloat16
 
 
@@ -175,6 +176,7 @@
 
 SUB = ROWS // 2
 CHUNK = HID // 2
+CUT = SUB // 2
 ANY = pl.BlockSpec(memory_space=pl.ANY)
 WHOLE = pl.BlockSpec(memory_space=pltpu.VMEM)
 SMEM = pl.BlockSpec(memory_space=pltpu.SMEM)
@@ -186,55 +188,54 @@
     return pl.ds(start, QUARTER)
 
 
-def project_kernel(parts_per_out, place, own, took, *refs):
-    count = sum(parts_per_out)
-    parts, outs = refs[:count], refs[count : count + len(parts_per_out)]
-    x_out, x, w, sems = refs[count + len(parts_per_out) :]
-    size = parts[0].shape[0]
-    copies = [
-        pltpu.make_async_copy(
-            own.at[pl.ds(0, SUB)], x.at[:, columns(place, False)], sems.at[0]
+def project_kernel(chunks, place, own, *refs):
+    took, refs = refs[:chunks], refs[chunks:]
+    parts, (out, x_out, x, w, sems) = refs[:-5], refs[-5:]
+    size, step = parts[0].shape[0], SUB // chunks
+    loads = [
+        pltpu.make_async_copy(own.at[pl.ds(0, SUB)], x.at[:, columns(place, False)], sems.at[0])
+    ]
+    for j, chunk in enumerate(took):
+        target = x.at[pl.ds(j * step, step), columns(place, True)]
+        loads.append(pltpu.make_async_copy(chunk, target, sems.at[2 + j]))
+    for j, part in enumerate(parts):
+        target = w.at[pl.ds(j * size, size)]
+        loads.append(pltpu.make_async_copy(part, target, sems.at[2 + chunks + j]))
+    for load in loads:
+        load.start()
+    for load in loads[: 1 + chunks]:
+        load.wait()
+    store = pltpu.make_async_copy(x, x_out, sems.at[1])
+    store.start()
+    halves = 2 if size > HID else 1
+    per = len(parts) // halves
+    for half in range(halves):
+        for load in loads[1 + chunks + half * per : 1 + chunks + (half + 1) * per]:
+            load.wait()
+        rows = slice(half * per * size, (half + 1) * per * size)
+        out[rows, :] = contract(w[rows, :], x[...], 1, 1).astype(BF16)
+    store.wait()
+
+
+def project(place, received, took, parts, name):
+    size, count = parts[0].shape[0], len(parts)
+    return pl.pallas_call(
+        functools.partial(project_kernel, len(took)),
+        out_shape=(
+            jax.ShapeDtypeStruct((count * size, SUB), BF16),
+            jax.ShapeDtypeStruct((SUB, HALF), BF16),
         ),
-        pltpu.make_async_copy(took, x.at[:, columns(place, True)], sems.at[1]),
-    ]
-    for j, part in enumerate(parts):
-        copies.append(
-            pltpu.make_async_copy(part, w.at[pl.ds(j * size, size)], sems.at[3 + j])
-        )
-    for copy in copies:
-        copy.start()
-    copies[0].wait()
-    copies[1].wait()
-    store = pltpu.make_async_copy(x, x_out, sems.at[2])
-    store.start()
-    for copy in copies[2:]:
-        copy.wait()
-    row = 0
-    for out, number in zip(outs, parts_per_out):
-        out[...] = contract(w[row : row + number * size, :], x[...], 1, 1).astype(BF16)
-        row += number * size
-    store.wait()
-
-
-def project(place, received, took, groups, name, micros):
-    parts = [part for group in groups for part in group]
-    size = parts[0].shape[0]
-    counts = tuple(len(group) for group in groups)
-    return pl.pallas_call(
-        functools.partial(project_kernel, counts),
-        out_shape=tuple(jax.ShapeDtypeStruct((size * n, SUB), BF16) for n in counts)
-        + (jax.ShapeDtypeStruct((SUB, HALF), BF16),),
-        in_specs=[SMEM] + [ANY] * (2 + len(parts)),
-        out_specs=(WHOLE,) * len(counts) + (ANY,),
+        in_specs=[SMEM] + [ANY] * (1 + len(took) + count),
+        out_specs=(WHOLE, ANY),
         scratch_shapes=[
             pltpu.VMEM((SUB, HALF), BF16),
-            pltpu.VMEM((len(parts) * size, HALF), BF16),
-            pltpu.SemaphoreType.DMA((3 + len(parts),)),
+            pltpu.VMEM((count * size, HALF), BF16),
+            pltpu.SemaphoreType.DMA((2 + len(took) + count,)),
         ],
         compiler_params=PARAMS,
-        cost_estimate=cost(micros),
+        cost_estimate=cost(SHORT),
         name=name,
-    )(place, received, took, *parts)
+    )(place, received, *took, *parts)
 
 
 def block(shape, row=0):
@@ -267,20 +268,14 @@
         sigma = jax.nn.sigmoid(gate)
         active = gate * sigma
         rows = pl.ds(j * HID, HID)
-        active_out[rows, :] = active
-        slope_out[rows, :] = up * sigma * (1.0 + gate * (1.0 - sigma))
+        active_out[rows, :] = active.astype(BF16)
+        slope_out[rows, :] = (up * sigma * (1.0 + gate * (1.0 - sigma))).astype(BF16)
         hidden[j] = (active * up).astype(BF16)
     hidden_here[:HID, :] = hidden[0]
     hidden_here[HID:, :] = hidden[1]
     total = contract(jnp.concatenate(hidden[2:], axis=0), dy[...], 1, 0).astype(BF16)
     for j, out in enumerate(grad_away):
         out[...] = total[j * CHUNK : (j + 1) * CHUNK]
-
-
-def here_kernel(rows, x, add, mine, there):
-    size = mine.shape[0]
-    mine[...] = contract(rows[:size, :], x[...], 1, 0) + add[:size, :].astype(F32)
-    there[...] = (contract(rows[size:, :], x[...], 1, 0) + add[size:, :].astype(F32)).astype(BF16)
 
 
 def down_here_kernel(rows, x, add0, add1, add2, add3, mine, there):
@@ -292,87 +287,127 @@
     there[CHUNK:, :] = (total[CHUNK:] + add3[...].astype(F32)).astype(BF16)
 
 
-def grad_here(rows, x, add, micros, name):
-    size = rows.shape[0] // 2
-    outs = [((size, HALF), F32), ((size, HALF), BF16)]
-    return single(here_kernel, outs, [full(rows), full(x), full(add)], micros, name)
-
-
-def away_kernel(rows, x, out):
-    out[...] = contract(rows[...], x[...], 1, 0).astype(BF16)
-
-
-def piece_kernel(
-    place, ours, theirs, active, slope, part0, part1, part2, part3, here, away, keep, give0, give1, w, sems
+def back_kernel(
+    place,
+    ours,
+    theirs,
+    active,
+    slope,
+    x_in,
+    part0,
+    part1,
+    part2,
+    part3,
+    give0,
+    give1,
+    keep,
+    far0,
+    far1,
+    far2,
+    far3,
+    there,
+    core,
+    mine,
+    x,
+    w,
+    both,
+    piece,
+    grads,
+    own,
+    sems,
 ):
-    copies = []
+    loads = [pltpu.make_async_copy(x_in, x, sems.at[4])]
     for j, part in enumerate((part0, part1, part2, part3)):
-        copies.append(
-            pltpu.make_async_copy(part, w.at[pl.ds(2 * j * HID, 2 * HID)], sems.at[j])
-        )
-    for copy in copies:
+        target = w.at[pl.ds(2 * j * HID, 2 * HID)]
+        loads.append(pltpu.make_async_copy(part, target, sems.at[j]))
+    for load in loads:
+        load.start()
+    for j in range(4):
+        rows = pl.ds(j * HID, HID)
+        grad = ours[rows, :].astype(F32) + theirs[rows, :].astype(F32)
+        both[pl.ds(2 * j * HID, HID), :] = (grad * slope[rows, :].astype(F32)).astype(BF16)
+        both[pl.ds((2 * j + 1) * HID, HID), :] = (grad * active[rows, :].astype(F32)).astype(BF16)
+    stores = []
+
+    def store(source, target):
+        copy = pltpu.make_async_copy(source, target, sems.at[5 + len(stores)])
         copy.start()
-    for out, low in ((here, 0), (away, 2)):
-        for j in range(2):
-            rows = pl.ds((low + j) * HID, HID)
-            grad = ours[rows, :].astype(F32) + theirs[rows, :].astype(F32)
-            out[pl.ds(2 * j * HID, HID), :] = (grad * slope[rows, :]).astype(BF16)
-            out[pl.ds((2 * j + 1) * HID, HID), :] = (grad * active[rows, :]).astype(BF16)
-    both = jnp.concatenate([here[...], away[...]], axis=0)
-    for copy in copies:
+        stores.append(copy)
+
+    loads[0].wait()
+    own[...] = contract(both[: 2 * HID, :], x[...], 1, 0)
+    store(own, mine)
+    grads[0] = contract(both[6 * HID :, :], x[...], 1, 0).astype(BF16)
+    for j, target in enumerate((far0, far1, far2, far3)):
+        store(grads.at[0, pl.ds(j * CHUNK, CHUNK)], target)
+    for slot, target in ((1, there), (2, core)):
+        rows = slice(slot * 2 * HID, (slot + 1) * 2 * HID)
+        grads[slot] = contract(both[rows, :], x[...], 1, 0).astype(BF16)
+        store(grads.at[slot], target)
+    for load in loads[1:]:
+        load.wait()
+    piece[1] = contract(both[...], w[:, columns(place, False)], 0, 0).astype(BF16)
+    store(piece.at[1], keep.at[pl.ds(0, SUB)])
+    for part, target in enumerate((give0, give1)):
+        rows = slice(part * CUT, (part + 1) * CUT)
+        piece[0, rows, :] = contract(both[:, rows], w[:, columns(place, True)], 0, 0).astype(BF16)
+        store(piece.at[0, pl.ds(part * CUT, CUT)], target)
+    for copy in stores:
         copy.wait()
-    total = contract(both, w[:, columns(place, True)], 0, 0).astype(BF16)
-    give0[...] = total[: SUB // 2]
-    give1[...] = total[SUB // 2 :]
-    keep[...] = contract(both, w[:, columns(place, False)], 0, 0).astype(BF16)
-
-
-def pieces(place, ours, theirs, active, slope, parts, micros):
-    outs = [(4 * HID, SUB)] * 2 + [(ROWS, QUARTER)] + [(SUB // 2, QUARTER)] * 2
-    blocks = [(4 * HID, SUB)] * 2 + [(SUB, QUARTER)] + [(SUB // 2, QUARTER)] * 2
+
+
+def back_products(place, ours, theirs, active, slope, x, parts):
+    outs = [((CUT, QUARTER), BF16)] * 2 + [((ROWS, QUARTER), BF16)]
+    outs += [((CHUNK, HALF), BF16)] * 4 + [((2 * HID, HALF), BF16)] * 2 + [((2 * HID, HALF), F32)]
     return pl.pallas_call(
-        piece_kernel,
+        back_kernel,
         grid=(1,),
-        out_shape=tuple(jax.ShapeDtypeStruct(shape, BF16) for shape in outs),
-        in_specs=[SMEM] + [block((4 * HID, SUB))] * 4 + [ANY] * 4,
-        out_specs=tuple(block(shape) for shape in blocks),
+        out_shape=tuple(jax.ShapeDtypeStruct(shape, kind) for shape, kind in outs),
+        in_specs=[SMEM] + [block((4 * HID, SUB))] * 4 + [ANY] * 5,
+        out_specs=(ANY,) * 10,
         scratch_shapes=[
+            pltpu.VMEM((SUB, HALF), BF16),
             pltpu.VMEM((8 * HID, HALF), BF16),
-            pltpu.SemaphoreType.DMA((4,)),
+            pltpu.VMEM((8 * HID, SUB), BF16),
+            pltpu.VMEM((2, SUB, QUARTER), BF16),
+            pltpu.VMEM((3, 2 * HID, HALF), BF16),
+            pltpu.VMEM((2 * HID, HALF), F32),
+            pltpu.SemaphoreType.DMA((15,)),
         ],
         compiler_params=PARAMS,
-        cost_estimate=cost(micros),
-        name="pieces",
-    )(place, ours, theirs, active, slope, *parts)
-
-
-def adam_kernel(weight, first, second, mine, took, new_weight, new_first, new_second):
-    grad = mine[...] + took[...].astype(F32)
+        cost_estimate=cost(SHORT),
+        name="back_products",
+    )(place, ours, theirs, active, slope, x, *parts)
+
+
+def adam_kernel(terms, weight, first, second, *refs):
+    new_weight, new_first, new_second = refs[-3:]
+    grad = refs[0][...].astype(F32)
+    for term in refs[1:terms]:
+        grad += term[...].astype(F32)
     new_weight[...], new_first[...], new_second[...] = adam_step(
         weight[...], first[...], second[...], grad
     )
 
 
-def adam(weight, first, second, mine, took, micros, name):
-    rows = mine.shape[0]
+def adam(weight, first, second, terms, took, name, flops=1):
     step = 32
+    flat = (took.shape[0], HALF)
     spec = pl.BlockSpec((step, HALF), lambda i: (i, 0))
-    flat = (rows, HALF)
-    outs = pl.pallas_call(
-        adam_kernel,
-        grid=(rows // step,),
+    return pl.pallas_call(
+        functools.partial(adam_kernel, len(terms) + 1),
+        grid=(flat[0] // step,),
         out_shape=(
             jax.ShapeDtypeStruct(flat, BF16),
             jax.ShapeDtypeStruct(flat, F32),
             jax.ShapeDtypeStruct(flat, F32),
         ),
-        in_specs=[spec] * 5,
+        in_specs=[spec] * (4 + len(terms)),
         out_specs=(spec,) * 3,
         compiler_params=pltpu.CompilerParams(vmem_limit_bytes=16 * 1024 * 1024),
-        cost_estimate=cost(micros),
+        cost_estimate=pl.CostEstimate(flops=flops, bytes_accessed=1, transcendentals=0),
         name=name,
-    )(weight.reshape(flat), first.reshape(flat), second.reshape(flat), mine, took)
-    return [out.reshape(weight.shape) for out in outs]
+    )(weight.reshape(flat), first.reshape(flat), second.reshape(flat), *terms, took)
 
 
 def per_device(
@@ -412,19 +447,19 @@
     got_dy = exchange(send_dy)
 
     gu_parts = (own_gu, y_gu, core_gu, far_gu)
-    part_gu, row_x = project(place, got_x, took_x, [gu_parts], "project_gate_up", 10)
+    part_gu, row_x = project(place, got_x, [took_x], gu_parts, "project_gate_up")
     there_gu = from_partner(part_gu, "ep", 1)
     late_dy, _ = lax.optimization_barrier((got_dy, part_gu))
     took_dy = from_partner(late_dy[SUB:], "rep", 1)
     part_hg, row_dy = project(
-        place, late_dy, took_dy, [(own_down, y_down, core_down, far_down)], "project_down", 7
+        place, late_dy, [took_dy], (own_down, y_down, core_down, far_down), "project_down"
     )
     there_hg = from_partner(part_hg, "ep", 1)
 
     half = (2 * HID, SUB)
     active, slope, hidden_here, *down_away = single(
         hidden_kernel,
-        [((4 * HID, SUB), F32), ((4 * HID, SUB), F32), (half, BF16)]
+        [((4 * HID, SUB), BF16), ((4 * HID, SUB), BF16), (half, BF16)]
         + [((CHUNK, HALF), BF16)] * 4,
         [full(part_gu), full(there_gu), full(row_dy)],
         SHORT,
@@ -440,35 +475,42 @@
     )
     active, slope, down_send = lax.optimization_barrier((active, slope, down_send))
     down_there = from_partner(down_send, "rep", 2)
-    both_here, both_away, keep, *give = pieces(
-        place, part_hg, there_hg, active, slope, gu_parts, SHORT
-    )
-    took_give = [from_partner(chunk, "rep", 1) for chunk in give]
-    (away,) = single(
-        away_kernel, [((4 * HID, HALF), BF16)], [full(both_away), full(row_x)], SHORT, "grad_away"
-    )
-    took_give, away, down_there = lax.optimization_barrier((took_give, away, down_there))
+    give0, give1, keep, *far, there, toward_core, mine = back_products(
+        place, part_hg, there_hg, active, slope, row_x, gu_parts
+    )
+    took_far = [from_partner(chunk, "rep", 1) for chunk in far]
+    send_there = (there.astype(F32) + jnp.concatenate(took_far).astype(F32)).astype(BF16)
+    gu_there = from_partner(send_there, "rep", 2)
+    took_give = [from_partner(chunk, "rep", 1) for chunk in (give0, give1)]
+    took_give, down_there = lax.optimization_barrier((took_give, down_there))
     for j, chunk in enumerate(took_give):
-        keep = lax.dynamic_update_slice(keep, chunk, (SUB + j * SUB // 2, 0))
+        keep = lax.dynamic_update_slice(keep, chunk, (SUB + j * CUT, 0))
+    toward_core, keep = lax.optimization_barrier((toward_core, keep))
     back = exchange(keep)
-    mine, there = grad_here(both_here, row_x, from_partner(away, "rep", 1), 7, "grad_here")
-    gu_there = from_partner(there, "rep", 2)
+    mine = mine + from_partner(toward_core, "rep", 1).astype(F32)
+    new_down, down_first, down_second = adam(
+        down_weight, down_m, down_v, (down_mine,), down_there, "adam_down"
+    )
     new_gu, gu_first, gu_second = adam(
-        gate_up_weight, gate_up_m, gate_up_v, mine, gu_there, 8, "adam_gate_up"
-    )
-    new_down, down_first, down_second = adam(
-        down_weight, down_m, down_v, down_mine, down_there, 4, "adam_down"
-    )
-
+        gate_up_weight, gate_up_m, gate_up_v, (mine,), gu_there, "adam_gate_up", UPDATE
+    )
+    back, new_gu = lax.optimization_barrier((back, new_gu))
     token_sum = contract(pick, back, 0, 0)
     lower, upper = token_sum[:TOK], token_sum[TOK:]
     keep_sum = jnp.where(y_hi == 0, lower, upper)
     give_sum = jnp.where(y_hi == 0, upper, lower).astype(BF16)
-    took_sum, new_gu, new_down = lax.optimization_barrier(
-        (from_partner(give_sum, "rep", 2), new_gu, new_down)
-    )
+    took_sum, new_down = lax.optimization_barrier((from_partner(give_sum, "rep", 2), new_down))
     token_grad = (keep_sum + took_sum.astype(F32)).astype(BF16)
-    return (token_grad, new_gu, new_down, gu_first, gu_second, down_first, down_second)
+    gu, down = gate_up_weight.shape, down_weight.shape
+    return (
+        token_grad,
+        new_gu.reshape(gu),
+        new_down.reshape(down),
+        gu_first.reshape(gu),
+        gu_second.reshape(gu),
+        down_first.reshape(down),
+        down_second.reshape(down),
+    )
 
 
 def solution(mesh):

time: 260 us -> 257 us (0.988)
  waiting for transfers between devices: 121 us -> 133 us
  Pallas kernels: 70 us -> 61 us
  local copies, waits for them, and re-layouts: 22.8 us -> 15.8 us
  other arithmetic: 0.93 us -> 4.48 us
    ppermute x20 -> x24, waiting for transfers between devices: 83 us -> 118 us  [from_partner(): return lax.ppermute(value, axis, pairs)]
    all_to_all x3, waiting for transfers between devices: 38 us -> 14.9 us  [exchange(): lax.all_to_all(value.reshape(N_EP, HALF_ROWS, QUARTER), ('ep', 'rep'), sp...]
    pallas_call x4 -> x2, Pallas kernels: 25.1 us -> 11.4 us  [single(): pl.pallas_call(kernel, grid=(1,), out_shape=tuple((jax.ShapeDtypeStruct(s...]
    unnamed x66 -> x64, local copies, waits for them, and re-layouts: 18.2 us -> 11.1 us
    pallas_call x5, Pallas kernels: 39.5 us -> 42.7 us  [the longest x2 18.6 us: project(): pl.pallas_call(functools.partial(project_kernel, len(took)), out_shape=(j...]
    add x0 -> x1, other arithmetic: none -> 3 us  [per_device(): mine = mine + from_partner(toward_core, 'rep', 1).astype(F32)]
    ppermute x20 -> x24, starting transfers between devices: 13.4 us -> 12.5 us  [from_partner(): return lax.ppermute(value, axis, pairs)]
  transfers between devices with their start and end apart: 23 -> 27, of which waited for: 15 -> 18; matrix products, arithmetic and copies ran while one was open for 3% -> 3% of each run, Pallas kernels for 27% -> 24%
where the time goes in v3:
time: 257 us; the launch traced here: 256 us
  waiting for transfers between devices  133 us (52%)
  Pallas kernels  61 us (24%)
  starting transfers between devices  38.4 us (15%)
  local copies, waits for them, and re-layouts  15.8 us (6%)
  other arithmetic  4.48 us (2%)
  matrix products  2.77 us (1%)
    ppermute x24, waiting for transfers between devices, from_partner(): return lax.ppermute(value, axis, pairs)  118 us
    all_to_all x3, starting transfers between devices, exchange(): lax.all_to_all(value.reshape(N_EP, HALF_ROWS, QUARTER), ('ep', 'rep'), sp...  25.9 us
    pallas_call x2, Pallas kernels, project(): pl.pallas_call(functools.partial(project_kernel, len(took)), out_shape=(j...  18.6 us
    all_to_all x3, waiting for transfers between devices, exchange(): lax.all_to_all(value.reshape(N_EP, HALF_ROWS, QUARTER), ('ep', 'rep'), sp...  14.9 us
    pallas_call x1, Pallas kernels, back_products(): pl.pallas_call(back_kernel, grid=(1,), out_shape=tuple((jax.ShapeDtypeStr...  14.1 us
    ppermute x24, starting transfers between devices, from_partner(): return lax.ppermute(value, axis, pairs)  12.5 us
    pallas_call x2, Pallas kernels, single(): pl.pallas_call(kernel, grid=(1,), out_shape=tuple((jax.ShapeDtypeStruct(s...  11.4 us
    unnamed x64, local copies, waits for them, and re-layouts  11.1 us
  transfers between devices with their start and end apart: 27, of which 18 were waited for; matrix products, arithmetic and copies ran while one was open for 3% of the time, Pallas kernels for 24%

profile of v3, /device:TPU:40, one launch (start us, length us, event | category | flops | bytes accessed | tf_op | source)
XLA Modules:
  0.0 256.5 jit_solution(4756369502649207494)
XLA Ops:
  0.6 2.4 collective-permute-start
  5.0 2.7 %send_tokens.1 = (bf16[1280,1024]{1,0:T(8,128)(2,1)S(1)}, bf16[1280,256]{1,0:T(8,128)(2,1)S(1)}) custom-call(s32[3]{0:T(128)S(1)} %pad_add_fusion.place, s32[8,128]{1,0:T(8,128)S(1)} %bitcast.38, bf16[128,4096]{1,0:T(8,128)(2,1)S(1)} %copy-done.2, bf16[128,4096]{1,0:T(8,128)(2,1)S(1)} %copy-done.2), custom_call_target="tpu_custom_call" | custom-call | flops 1 | bytes 3000000 | tf_op jit(solution)/shard_map/send_tokens/pallas_call | solution.py:162
  9.2 9.1 %all-to-all-start.1 = ((bf16[32,40,1024]{2,1,0:T(8,128)(2,1)}), bf16[32,40,1024]{2,1,0:T(8,128)(2,1)}, u32[]{:S(2)}, u32[]{:S(2)}) async-start(bf16[32,40,1024]{2,1,0:T(8,128)(2,1)} %bitcast.35), calls=%async_computation.1 | async-start | bytes 5242880 | tf_op jit(solution)/shard_map/all_to_all | solution.py:59
  18.4 33.9 %collective-permute-done.refs_2_.part1 = bf16[384,2048]{1,0:T(8,128)(2,1)} collective-permute-done((bf16[384,2048]{1,0:T(8,128)(2,1)}, bf16[384,2048]{1,0:T(8,128)(2,1)}, u32[]{:S(2)}, u32[]{:S(2)}) %collective-permute-start) | collective-permute-done | bytes 1572896 | tf_op jit(solution)/shard_map/ppermute | solution.py:42
  52.3 4.1 %send_grads.1 = bf16[1280,1024]{1,0:T(8,128)(2,1)} custom-call(s32[3]{0:T(128)S(1)} %pad_add_fusion.place, s32[8,128]{1,0:T(8,128)S(1)} %bitcast.39, f32[8,128]{1,0:T(8,128)S(1)} %bitcast.40, bf16[1280,256]{1,0:T(8,128)(2,1)S(1)} %get-tuple-element.53.pick_ref, bf16[128,4096]{1,0:T(8,128)(2,1)S(1)} %copy-done.3, bf16[128,4096]{1,0:T(8,128)(2,1)S(1)} %copy-done.3), custom_call_target="tpu_custom_call" | custom-call | flops 1 | bytes 3000000 | tf_op jit(solution)/shard_map/send_grads/pallas_call | solution.py:162
  57.3 7.9 %all-to-all-start = ((bf16[32,40,1024]{2,1,0:T(8,128)(2,1)}), bf16[32,40,1024]{2,1,0:T(8,128)(2,1)}, u32[]{:S(2)}, u32[]{:S(2)}) async-start(bf16[32,40,1024]{2,1,0:T(8,128)(2,1)} %bitcast.6), calls=%async_computation | async-start | bytes 5242880 | tf_op jit(solution)/shard_map/all_to_all | solution.py:59
  67.4 2.0 collective-permute-start.5
  71.8 11.6 %project_gate_up.1 = (bf16[1536,640]{1,0:T(8,128)(2,1)}, bf16[640,2048]{1,0:T(8,128)(2,1)}) custom-call(s32[3]{0:T(128)} %copy-done.14, bf16[1280,1024]{1,0:T(8,128)(2,1)} %bitcast.9.own, bf16[640,1024]{1,0:T(8,128)(2,1)} %copy-done.23, bf16[384,2048]{1,0:T(8,128)(2,1)} %bitcast.27, bf16[384,2048]{1,0:T(8,128)(2,1)} %collective-permute-done.refs_2_.part1, ...), custom_call_target="tpu_custom_call" | custom-call | flops 1 | bytes 30000 | tf_op jit(solution)/shard_map/project_gate_up/pallas_call | solution.py:222
  85.0 14.0 %all-to-all-done = bf16[32,40,1024]{2,1,0:T(8,128)(2,1)} async-done(((bf16[32,40,1024]{2,1,0:T(8,128)(2,1)}), bf16[32,40,1024]{2,1,0:T(8,128)(2,1)}, u32[]{:S(2)}, u32[]{:S(2)}) %all-to-all-start) | async-done | bytes 2621472 | tf_op jit(solution)/shard_map/all_to_all | solution.py:59
  101.0 2.3 collective-permute-done.5.refs_2_
  107.8 7.0 %project_down.1 = (bf16[768,640]{1,0:T(8,128)(2,1)}, bf16[640,2048]{1,0:T(8,128)(2,1)}) custom-call(s32[3]{0:T(128)} %copy-done.14, bf16[1280,1024]{1,0:T(8,128)(2,1)} %bitcast.7.own, bf16[640,1024]{1,0:T(8,128)(2,1)} %copy-done.22, bf16[192,2048]{1,0:T(8,128)(2,1)} %bitcast.31, bf16[192,2048]{1,0:T(8,128)(2,1)} %copy-done.25, bf16[192,2048]{1,0:T(8,128)(2,1)} %copy-done.26, ...), custom_call_target="tpu_custom_call" | custom-call | flops 1 | bytes 30000 | tf_op jit(solution)/shard_map/project_down/pallas_call | solution.py:222
  114.7 2.2 collective-permute-start.8
  117.0 25.1 %collective-permute-done.9.theirs = bf16[1536,640]{1,0:T(8,128)(2,1)S(1)} collective-permute-done((bf16[1536,640]{1,0:T(8,128)(2,1)}, bf16[1536,640]{1,0:T(8,128)(2,1)S(1)}, u32[]{:S(2)}, u32[]{:S(2)}) %collective-permute-start.9) | collective-permute-done | bytes 1966112 | tf_op jit(solution)/shard_map/ppermute | solution.py:42
  143.4 6.9 %hidden_and_down.1 = (bf16[768,640]{1,0:T(8,128)(2,1)}, bf16[768,640]{1,0:T(8,128)(2,1)}, bf16[384,640]{1,0:T(8,128)(2,1)}, bf16[96,2048]{1,0:T(8,128)(2,1)}, bf...) custom-call(bf16[1536,640]{1,0:T(8,128)(2,1)} %get-tuple-element.57.ours, ...), custom_call_target="tpu_custom_call" | custom-call | flops 1 | bytes 30000 | tf_op jit(solution)/shard_map/hidden_and_down/pallas_call | solution.py:246
  154.7 4.6 %down_here.1 = (f32[192,2048]{1,0:T(8,128)}, bf16[192,2048]{1,0:T(8,128)(2,1)}) custom-call(bf16[384,640]{1,0:T(8,128)(2,1)} %get-tuple-element.63.rows, bf16[640,2048]{1,0:T(8,128)(2,1)} %get-tuple-element.60.dy.x, bf16[96,2048]{1,0:T(8,128)(2,1)} %copy-done.28, bf16[96,2048]{1,0:T(8,128)(2,1)} %copy-done.29, bf16[96,2048]{1,0:T(8,128)(2,1)} %copy-done.30, ...), custom_call_target="tpu_custom_call" | custom-call | flops 1 | bytes 30000 | tf_op jit(solution)/shard_map/down_here/pallas_call | solution.py:246
  159.3 3.8 %collective-permute-done.8.theirs = bf16[768,640]{1,0:T(8,128)(2,1)S(1)} collective-permute-done((bf16[768,640]{1,0:T(8,128)(2,1)}, bf16[768,640]{1,0:T(8,128)(2,1)S(1)}, u32[]{:S(2)}, u32[]{:S(2)}) %collective-permute-start.8) | collective-permute-done | bytes 983072 | tf_op jit(solution)/shard_map/ppermute | solution.py:42
  164.0 14.1 %back_products.1 = (bf16[320,1024]{1,0:T(8,128)(2,1)}, bf16[320,1024]{1,0:T(8,128)(2,1)}, bf16[1280,1024]{1,0:T(8,128)(2,1)}, bf16[96,2048]{1,0:T(8,128)(2,1)}, ...) custom-call(s32[3]{0:T(128)} %copy-done.14, ...), custom_call_target="tpu_custom_call" | custom-call | flops 1 | bytes 30000 | tf_op jit(solution)/shard_map/back_products/pallas_call | solution.py:362
  184.4 8.9 %all-to-all-start.2 = ((bf16[32,40,1024]{2,1,0:T(8,128)(2,1)}), bf16[32,40,1024]{2,1,0:T(8,128)(2,1)}, u32[]{:S(2)}, u32[]{:S(2)}) async-start(bf16[32,40,1024]{2,1,0:T(8,128)(2,1)} %bitcast.43), calls=%async_computation.2 | async-start | bytes 5242880 | tf_op jit(solution)/shard_map/all_to_all | solution.py:59
  193.3 3.0 %convert_add_fusion.refs_0_ = f32[384,2048]{1,0:T(8,128)S(1)} fusion(f32[384,2048]{1,0:T(8,128)} %get-tuple-element.80, bf16[384,2048]{1,0:T(8,128)(2,1)} %collective-permute-done.17), kind=kLoop, calls=%fused_computation.1 | loop fusion | flops 1572864 | bytes 7864320 | tf_op jit(solution)/shard_map/add | solution.py:490
  196.3 40.8 %collective-permute-done.22.refs_1_ = bf16[384,2048]{1,0:T(8,128)(2,1)S(1)} collective-permute-done((bf16[384,2048]{1,0:T(8,128)(2,1)S(1)}, bf16[384,2048]{1,0:T(8,128)(2,1)S(1)}, u32[]{:S(2)}, u32[]{:S(2)}) %collective-permute-start.22) | collective-permute-done | bytes 1572896 | tf_op jit(solution)/shard_map/ppermute | solution.py:42
  237.1 6.6 %adam_gate_up.1 = (bf16[384,2048]{1,0:T(8,128)(2,1)}, f32[384,2048]{1,0:T(8,128)}, f32[384,2048]{1,0:T(8,128)}) custom-call(bf16[384,2048]{1,0:T(8,128)(2,1)S(1)} %bitcast.30, f32[384,2048]{1,0:T(8,128)S(1)} %bitcast.41, f32[384,2048]{1,0:T(8,128)S(1)} %bitcast.42, f32[384,2048]{1,0:T(8,128)S(1)} %convert_add_fusion.refs_0_, ...), custom_call_target="tpu_custom_call" | custom-call | flops 4999999913984 | bytes 1 | tf_op jit(solution)/shard_map/adam_gate_up/pallas_call | solution.py:397
  243.7 2.8 %fusion = f32[256,1024]{1,0:T(8,128)S(1)} fusion(bf16[1280,256]{1,0:T(8,128)(2,1)S(1)} %copy-done.13, bf16[1280,1024]{1,0:T(8,128)(2,1)} %bitcast.13), kind=kOutput, calls=%fused_computation.7 | convolution fusion | flops 671088640 | bytes 4325376 | tf_op jit(solution)/shard_map/dot_general | solution.py:70
  248.2 3.4 %adam_down.1 = (bf16[192,2048]{1,0:T(8,128)(2,1)}, f32[192,2048]{1,0:T(8,128)}, f32[192,2048]{1,0:T(8,128)}) custom-call(bf16[192,2048]{1,0:T(8,128)(2,1)S(1)} %bitcast.34, f32[192,2048]{1,0:T(8,128)S(1)} %bitcast.36, f32[192,2048]{1,0:T(8,128)S(1)} %bitcast.37, f32[192,2048]{1,0:T(8,128)S(1)} %copy-done.9, bf16[192,2048]{1,0:T(8,128)(2,1)S(1)} %copy-done.11), custom_call_target="tpu_custom_call" | custom-call | flops 1 | bytes 1 | tf_op jit(solution)/shard_map/adam_down/pallas_call | solution.py:397
  251.7 4.0 %collective-permute-done.23 = bf16[128,1024]{1,0:T(8,128)(2,1)S(1)} collective-permute-done((bf16[128,1024]{1,0:T(8,128)(2,1)S(1)}, bf16[128,1024]{1,0:T(8,128)(2,1)S(1)}, u32[]{:S(2)}, u32[]{:S(2)}) %collective-permute-start.23) | collective-permute-done | bytes 262176 | tf_op jit(solution)/shard_map/ppermute | solution.py:42
  (113 shorter events, 32.4 us)
Async XLA Ops:
  0.6 51.6 %collective-permute-start = (bf16[384,2048]{1,0:T(8,128)(2,1)}, bf16[384,2048]{1,0:T(8,128)(2,1)}, u32[]{:S(2)}, u32[]{:S(2)}) collective-permute-start(bf16[384,2048]{1,0:T(8,128)(2,1)} %bitcast.26), channel_id=1, source_target_pairs={{0,2},{1,3},{2,0},{3,1},{4,6},{5,7},{6,4},{7,5},{8,10},{9,11},{10,... | collective-permute-start | bytes 4718600 | tf_op jit(solution)/shard_map/ppermute | solution.py:42
  9.2 48.0 %all-to-all-start.1 = ((bf16[32,40,1024]{2,1,0:T(8,128)(2,1)}), bf16[32,40,1024]{2,1,0:T(8,128)(2,1)}, u32[]{:S(2)}, u32[]{:S(2)}) async-start(bf16[32,40,1024]{2,1,0:T(8,128)(2,1)} %bitcast.35), calls=%async_computation.1 | async-start | bytes 5242880 | tf_op jit(solution)/shard_map/all_to_all | solution.py:59
  52.2 4.1 %collective-permute-start.1 = (bf16[384,2048]{1,0:T(8,128)(2,1)}, bf16[384,2048]{1,0:T(8,128)(2,1)}, u32[]{:S(2)}, u32[]{:S(2)}) collective-permute-start(bf16[384,2048]{1,0:T(8,128)(2,1)} %collective-permute-done.refs_2_.part1), channel_id=1, source_target_pairs={{0,1},{1,0},{2,3},{3,2},{4,5},{5,4},{6,7},{7,6},{8,9},{9,8},{10,11... | collective-permute-start | bytes 4718600 | tf_op jit(solution)/shard_map/ppermute | solution.py:42
  57.3 41.8 %all-to-all-start = ((bf16[32,40,1024]{2,1,0:T(8,128)(2,1)}), bf16[32,40,1024]{2,1,0:T(8,128)(2,1)}, u32[]{:S(2)}, u32[]{:S(2)}) async-start(bf16[32,40,1024]{2,1,0:T(8,128)(2,1)} %bitcast.6), calls=%async_computation | async-start | bytes 5242880 | tf_op jit(solution)/shard_map/all_to_all | solution.py:59
  65.2 4.3 %collective-permute-start.3 = (bf16[384,2048]{1,0:T(8,128)(2,1)S(1)}, bf16[384,2048]{1,0:T(8,128)(2,1)S(1)}, u32[]{:S(2)}, u32[]{:S(2)}) collective-permute-start(bf16[384,2048]{1,0:T(8,128)(2,1)S(1)} %bitcast.29), channel_id=1, source_target_pairs={{0,1},{1,0},{2,3},{3,2},{4,5},{5,4},{6,7},{7,6},{8,9},{9,8},{10,11... | collective-permute-start | bytes 4718600 | tf_op jit(solution)/shard_map/ppermute | solution.py:42
  67.3 3.5 %collective-permute-start.2 = (bf16[640,1024]{1,0:T(8,128)(2,1)S(1)}, bf16[640,1024]{1,0:T(8,128)(2,1)S(1)}, u32[]{:S(2)}, u32[]{:S(2)}) collective-permute-start(bf16[640,1024]{1,0:T(8,128)(2,1)S(1)} %bitcast.44), channel_id=1, source_target_pairs={{0,1},{1,0},{2,3},{3,2},{4,5},{5,4},{6,7},{7,6},{8,9},{9,8},{10,11... | collective-permute-start | bytes 3932168 | tf_op jit(solution)/shard_map/ppermute | solution.py:42
  67.4 35.9 %collective-permute-start.5 = (bf16[192,2048]{1,0:T(8,128)(2,1)S(1)}, bf16[192,2048]{1,0:T(8,128)(2,1)S(1)}, u32[]{:S(2)}, u32[]{:S(2)}) collective-permute-start(bf16[192,2048]{1,0:T(8,128)(2,1)S(1)} %bitcast.32), channel_id=1, source_target_pairs={{0,2},{1,3},{2,0},{3,1},{4,6},{5,7},{6,4},{7,5},{8,10},{9,11},{10,... | collective-permute-start | bytes 2359304 | tf_op jit(solution)/shard_map/ppermute | solution.py:42
  83.4 58.6 %collective-permute-start.9 = (bf16[1536,640]{1,0:T(8,128)(2,1)}, bf16[1536,640]{1,0:T(8,128)(2,1)S(1)}, u32[]{:S(2)}, u32[]{:S(2)}) collective-permute-start(bf16[1536,640]{1,0:T(8,128)(2,1)} %get-tuple-element.57.ours), channel_id=1, source_target_pairs={{0,4},{4,0},{8,12},{12,8},{16,20},{20,16},{24,28},{28,24},{32,36},... | collective-permute-start | bytes 5898248 | tf_op jit(solution)/shard_map/ppermute | solution.py:42
  100.4 5.4 %collective-permute-start.4 = (bf16[640,1024]{1,0:T(8,128)(2,1)S(1)}, bf16[640,1024]{1,0:T(8,128)(2,1)S(1)}, u32[]{:S(2)}, u32[]{:S(2)}) collective-permute-start(bf16[640,1024]{1,0:T(8,128)(2,1)S(1)} %slice.17), channel_id=1, source_target_pairs={{0,1},{1,0},{2,3},{3,2},{4,5},{5,4},{6,7},{7,6},{8,9},{9,8},{10,11... | collective-permute-start | bytes 3932168 | tf_op jit(solution)/shard_map/ppermute | solution.py:42
  100.5 4.1 %collective-permute-start.6 = (bf16[192,2048]{1,0:T(8,128)(2,1)S(1)}, bf16[192,2048]{1,0:T(8,128)(2,1)S(1)}, u32[]{:S(2)}, u32[]{:S(2)}) collective-permute-start(bf16[192,2048]{1,0:T(8,128)(2,1)S(1)} %bitcast.33), channel_id=1, source_target_pairs={{0,1},{1,0},{2,3},{3,2},{4,5},{5,4},{6,7},{7,6},{8,9},{9,8},{10,11... | collective-permute-start | bytes 2359304 | tf_op jit(solution)/shard_map/ppermute | solution.py:42
  114.7 48.3 %collective-permute-start.8 = (bf16[768,640]{1,0:T(8,128)(2,1)}, bf16[768,640]{1,0:T(8,128)(2,1)S(1)}, u32[]{:S(2)}, u32[]{:S(2)}) collective-permute-start(bf16[768,640]{1,0:T(8,128)(2,1)} %get-tuple-element.59.ours), channel_id=1, source_target_pairs={{0,4},{4,0},{8,12},{12,8},{16,20},{20,16},{24,28},{28,24},{32,36},... | collective-permute-start | bytes 2949128 | tf_op jit(solution)/shard_map/ppermute | solution.py:42
  150.3 2.5 collective-permute-start.11
  150.8 2.5 collective-permute-start.12
  150.9 3.0 %collective-permute-start.13 = (bf16[96,2048]{1,0:T(8,128)(2,1)}, bf16[96,2048]{1,0:T(8,128)(2,1)S(1)}, u32[]{:S(2)}, u32[]{:S(2)}) collective-permute-start(bf16[96,2048]{1,0:T(8,128)(2,1)} %get-tuple-element.67), channel_id=1, source_target_pairs={{0,1},{1,0},{2,3},{3,2},{4,5},{5,4},{6,7},{7,6},{8,9},{9,8},{10,11... | collective-permute-start | bytes 1179656 | tf_op jit(solution)/shard_map/ppermute | solution.py:42
  159.2 21.3 %collective-permute-start.16 = (bf16[192,2048]{1,0:T(8,128)(2,1)}, bf16[192,2048]{1,0:T(8,128)(2,1)S(1)}, u32[]{:S(2)}, u32[]{:S(2)}) collective-permute-start(bf16[192,2048]{1,0:T(8,128)(2,1)} %get-tuple-element.76), channel_id=1, source_target_pairs={{0,2},{1,3},{2,0},{3,1},{4,6},{5,7},{6,4},{7,5},{8,10},{9,11},{10,... | collective-permute-start | bytes 2359304 | tf_op jit(solution)/shard_map/ppermute | solution.py:42
  178.2 3.2 %collective-permute-start.15 = (bf16[320,1024]{1,0:T(8,128)(2,1)}, bf16[320,1024]{1,0:T(8,128)(2,1)S(1)}, u32[]{:S(2)}, u32[]{:S(2)}) collective-permute-start(bf16[320,1024]{1,0:T(8,128)(2,1)} %get-tuple-element.75), channel_id=1, source_target_pairs={{0,1},{1,0},{2,3},{3,2},{4,5},{5,4},{6,7},{7,6},{8,9},{9,8},{10,11... | collective-permute-start | bytes 1966088 | tf_op jit(solution)/shard_map/ppermute | solution.py:42
  178.7 4.7 %collective-permute-start.18 = (bf16[96,2048]{1,0:T(8,128)(2,1)}, bf16[96,2048]{1,0:T(8,128)(2,1)S(1)}, u32[]{:S(2)}, u32[]{:S(2)}) collective-permute-start(bf16[96,2048]{1,0:T(8,128)(2,1)} %get-tuple-element.83), channel_id=1, source_target_pairs={{0,1},{1,0},{2,3},{3,2},{4,5},{5,4},{6,7},{7,6},{8,9},{9,8},{10,11... | collective-permute-start | bytes 1179656 | tf_op jit(solution)/shard_map/ppermute | solution.py:42
  178.8 4.6 %collective-permute-start.19 = (bf16[96,2048]{1,0:T(8,128)(2,1)}, bf16[96,2048]{1,0:T(8,128)(2,1)S(1)}, u32[]{:S(2)}, u32[]{:S(2)}) collective-permute-start(bf16[96,2048]{1,0:T(8,128)(2,1)} %get-tuple-element.84), channel_id=1, source_target_pairs={{0,1},{1,0},{2,3},{3,2},{4,5},{5,4},{6,7},{7,6},{8,9},{9,8},{10,11... | collective-permute-start | bytes 1179656 | tf_op jit(solution)/shard_map/ppermute | solution.py:42
  180.5 2.9 %collective-permute-start.20 = (bf16[96,2048]{1,0:T(8,128)(2,1)}, bf16[96,2048]{1,0:T(8,128)(2,1)S(1)}, u32[]{:S(2)}, u32[]{:S(2)}) collective-permute-start(bf16[96,2048]{1,0:T(8,128)(2,1)} %get-tuple-element.85), channel_id=1, source_target_pairs={{0,1},{1,0},{2,3},{3,2},{4,5},{5,4},{6,7},{7,6},{8,9},{9,8},{10,11... | collective-permute-start | bytes 1179656 | tf_op jit(solution)/shard_map/ppermute | solution.py:42
  180.6 3.1 %collective-permute-start.21 = (bf16[96,2048]{1,0:T(8,128)(2,1)}, bf16[96,2048]{1,0:T(8,128)(2,1)S(1)}, u32[]{:S(2)}, u32[]{:S(2)}) collective-permute-start(bf16[96,2048]{1,0:T(8,128)(2,1)} %get-tuple-element.86), channel_id=1, source_target_pairs={{0,1},{1,0},{2,3},{3,2},{4,5},{5,4},{6,7},{7,6},{8,9},{9,8},{10,11... | collective-permute-start | bytes 1179656 | tf_op jit(solution)/shard_map/ppermute | solution.py:42
  183.3 10.0 %collective-permute-start.17 = (bf16[384,2048]{1,0:T(8,128)(2,1)}, bf16[384,2048]{1,0:T(8,128)(2,1)}, u32[]{:S(2)}, u32[]{:S(2)}) collective-permute-start(bf16[384,2048]{1,0:T(8,128)(2,1)} %get-tuple-element.81), channel_id=1, source_target_pairs={{0,1},{1,0},{2,3},{3,2},{4,5},{5,4},{6,7},{7,6},{8,9},{9,8},{10,11... | collective-permute-start | bytes 4718600 | tf_op jit(solution)/shard_map/ppermute | solution.py:42
  184.3 52.8 %collective-permute-start.22 = (bf16[384,2048]{1,0:T(8,128)(2,1)S(1)}, bf16[384,2048]{1,0:T(8,128)(2,1)S(1)}, u32[]{:S(2)}, u32[]{:S(2)}) collective-permute-start(bf16[384,2048]{1,0:T(8,128)(2,1)S(1)} %add_convert_fusion), channel_id=1, source_target_pairs={{0,2},{1,3},{2,0},{3,1},{4,6},{5,7},{6,4},{7,5},{8,10},{9,11},{10,... | collective-permute-start | bytes 4718600 | tf_op jit(solution)/shard_map/ppermute | solution.py:42
  184.4 59.3 %all-to-all-start.2 = ((bf16[32,40,1024]{2,1,0:T(8,128)(2,1)}), bf16[32,40,1024]{2,1,0:T(8,128)(2,1)}, u32[]{:S(2)}, u32[]{:S(2)}) async-start(bf16[32,40,1024]{2,1,0:T(8,128)(2,1)} %bitcast.43), calls=%async_computation.2 | async-start | bytes 5242880 | tf_op jit(solution)/shard_map/all_to_all | solution.py:59
  246.6 9.1 %collective-permute-start.23 = (bf16[128,1024]{1,0:T(8,128)(2,1)S(1)}, bf16[128,1024]{1,0:T(8,128)(2,1)S(1)}, u32[]{:S(2)}, u32[]{:S(2)}) collective-permute-start(bf16[128,1024]{1,0:T(8,128)(2,1)S(1)} %select_convert_fusion), channel_id=1, source_target_pairs={{0,2},{1,3},{2,0},{3,1},{4,6},{5,7},{6,4},{7,5},{8,10},{9,11},{10,... | collective-permute-start | bytes 786440 | tf_op jit(solution)/shard_map/ppermute | solution.py:42
  (35 other events, 373.9 us)

commit v4 on v3

--- a/solution.py
+++ b/solution.py
@@ -335,7 +335,7 @@
         stores.append(copy)
 
     loads[0].wait()
-    own[...] = contract(both[: 2 * HID, :], x[...], 1, 0)
+    own[...] = contract(both[: 2 * HID, :], x[...], 1, 0).astype(BF16)
     store(own, mine)
     grads[0] = contract(both[6 * HID :, :], x[...], 1, 0).astype(BF16)
     for j, target in enumerate((far0, far1, far2, far3)):
@@ -358,7 +358,7 @@
 
 def back_products(place, ours, theirs, active, slope, x, parts):
     outs = [((CUT, QUARTER), BF16)] * 2 + [((ROWS, QUARTER), BF16)]
-    outs += [((CHUNK, HALF), BF16)] * 4 + [((2 * HID, HALF), BF16)] * 2 + [((2 * HID, HALF), F32)]
+    outs += [((CHUNK, HALF), BF16)] * 4 + [((2 * HID, HALF), BF16)] * 3
     return pl.pallas_call(
         back_kernel,
         grid=(1,),
@@ -371,7 +371,7 @@
             pltpu.VMEM((8 * HID, SUB), BF16),
             pltpu.VMEM((2, SUB, QUARTER), BF16),
             pltpu.VMEM((3, 2 * HID, HALF), BF16),
-            pltpu.VMEM((2 * HID, HALF), F32),
+            pltpu.VMEM((2 * HID, HALF), BF16),
             pltpu.SemaphoreType.DMA((15,)),
         ],
         compiler_params=PARAMS,
@@ -391,7 +391,7 @@
 
 
 def adam(weight, first, second, terms, took, name, flops=1):
-    step = 32
+    step = 64
     flat = (took.shape[0], HALF)
     spec = pl.BlockSpec((step, HALF), lambda i: (i, 0))
     return pl.pallas_call(
@@ -487,7 +487,7 @@
         keep = lax.dynamic_update_slice(keep, chunk, (SUB + j * CUT, 0))
     toward_core, keep = lax.optimization_barrier((toward_core, keep))
     back = exchange(keep)
-    mine = mine + from_partner(toward_core, "rep", 1).astype(F32)
+    mine = mine.astype(F32) + from_partner(toward_core, "rep", 1).astype(F32)
     new_down, down_first, down_second = adam(
         down_weight, down_m, down_v, (down_mine,), down_there, "adam_down"
     )

time: 257 us -> 259 us (level)
    unnamed x64 -> x66, local copies, waits for them, and re-layouts: 11.1 us -> 13 us
  transfers between devices with their start and end apart: 27 -> 27, of which waited for: 18 -> 18; matrix products, arithmetic and copies ran while one was open for 3% -> 3% of each run, Pallas kernels for 24% -> 23%
where the time goes in v4:
time: 259 us; the launch traced here: 258 us
  waiting for transfers between devices  135 us (52%)
  Pallas kernels  58.8 us (23%)
  starting transfers between devices  38.5 us (15%)
  local copies, waits for them, and re-layouts  17.7 us (7%)
  other arithmetic  4.75 us (2%)
  matrix products  2.76 us (1%)
    ppermute x24, waiting for transfers between devices, from_partner(): return lax.ppermute(value, axis, pairs)  120 us
    all_to_all x3, starting transfers between devices, exchange(): lax.all_to_all(value.reshape(N_EP, HALF_ROWS, QUARTER), ('ep', 'rep'), sp...  26 us
    pallas_call x2, Pallas kernels, project(): pl.pallas_call(functools.partial(project_kernel, len(took)), out_shape=(j...  18.6 us
    all_to_all x3, waiting for transfers between devices, exchange(): lax.all_to_all(value.reshape(N_EP, HALF_ROWS, QUARTER), ('ep', 'rep'), sp...  14.9 us
    pallas_call x1, Pallas kernels, back_products(): pl.pallas_call(back_kernel, grid=(1,), out_shape=tuple((jax.ShapeDtypeStr...  14.1 us
    unnamed x66, local copies, waits for them, and re-layouts  13 us
    ppermute x24, starting transfers between devices, from_partner(): return lax.ppermute(value, axis, pairs)  12.4 us
    pallas_call x2, Pallas kernels, single(): pl.pallas_call(kernel, grid=(1,), out_shape=tuple((jax.ShapeDtypeStruct(s...  11.4 us
  transfers between devices with their start and end apart: 27, of which 18 were waited for; matrix products, arithmetic and copies ran while one was open for 3% of the time, Pallas kernels for 23%

profile of v4, /device:TPU:40, one launch (start us, length us, event | category | flops | bytes accessed | tf_op | source)
XLA Modules:
  0.0 258.0 jit_solution(7961906464071330464)
XLA Ops:
  0.6 2.4 collective-permute-start
  5.0 2.7 %send_tokens.1 = (bf16[1280,1024]{1,0:T(8,128)(2,1)S(1)}, bf16[1280,256]{1,0:T(8,128)(2,1)S(1)}) custom-call(s32[3]{0:T(128)S(1)} %pad_add_fusion.place, s32[8,128]{1,0:T(8,128)S(1)} %bitcast.38, bf16[128,4096]{1,0:T(8,128)(2,1)S(1)} %copy-done.2, bf16[128,4096]{1,0:T(8,128)(2,1)S(1)} %copy-done.2), custom_call_target="tpu_custom_call" | custom-call | flops 1 | bytes 3000000 | tf_op jit(solution)/shard_map/send_tokens/pallas_call | solution.py:162
  9.2 9.1 %all-to-all-start.1 = ((bf16[32,40,1024]{2,1,0:T(8,128)(2,1)}), bf16[32,40,1024]{2,1,0:T(8,128)(2,1)}, u32[]{:S(2)}, u32[]{:S(2)}) async-start(bf16[32,40,1024]{2,1,0:T(8,128)(2,1)} %bitcast.35), calls=%async_computation.1 | async-start | bytes 5242880 | tf_op jit(solution)/shard_map/all_to_all | solution.py:59
  18.4 33.9 %collective-permute-done.refs_2_.part1 = bf16[384,2048]{1,0:T(8,128)(2,1)} collective-permute-done((bf16[384,2048]{1,0:T(8,128)(2,1)}, bf16[384,2048]{1,0:T(8,128)(2,1)}, u32[]{:S(2)}, u32[]{:S(2)}) %collective-permute-start) | collective-permute-done | bytes 1572896 | tf_op jit(solution)/shard_map/ppermute | solution.py:42
  52.3 4.1 %send_grads.1 = bf16[1280,1024]{1,0:T(8,128)(2,1)} custom-call(s32[3]{0:T(128)S(1)} %pad_add_fusion.place, s32[8,128]{1,0:T(8,128)S(1)} %bitcast.39, f32[8,128]{1,0:T(8,128)S(1)} %bitcast.40, bf16[1280,256]{1,0:T(8,128)(2,1)S(1)} %get-tuple-element.53.pick_ref, bf16[128,4096]{1,0:T(8,128)(2,1)S(1)} %copy-done.3, bf16[128,4096]{1,0:T(8,128)(2,1)S(1)} %copy-done.3), custom_call_target="tpu_custom_call" | custom-call | flops 1 | bytes 3000000 | tf_op jit(solution)/shard_map/send_grads/pallas_call | solution.py:162
  57.3 7.9 %all-to-all-start = ((bf16[32,40,1024]{2,1,0:T(8,128)(2,1)}), bf16[32,40,1024]{2,1,0:T(8,128)(2,1)}, u32[]{:S(2)}, u32[]{:S(2)}) async-start(bf16[32,40,1024]{2,1,0:T(8,128)(2,1)} %bitcast.6), calls=%async_computation | async-start | bytes 5242880 | tf_op jit(solution)/shard_map/all_to_all | solution.py:59
  67.4 2.0 collective-permute-start.5
  71.8 11.6 %project_gate_up.1 = (bf16[1536,640]{1,0:T(8,128)(2,1)}, bf16[640,2048]{1,0:T(8,128)(2,1)}) custom-call(s32[3]{0:T(128)} %copy-done.14, bf16[1280,1024]{1,0:T(8,128)(2,1)} %bitcast.9.own, bf16[640,1024]{1,0:T(8,128)(2,1)} %copy-done.24, bf16[384,2048]{1,0:T(8,128)(2,1)} %bitcast.27, bf16[384,2048]{1,0:T(8,128)(2,1)} %collective-permute-done.refs_2_.part1, ...), custom_call_target="tpu_custom_call" | custom-call | flops 1 | bytes 30000 | tf_op jit(solution)/shard_map/project_gate_up/pallas_call | solution.py:222
  85.0 14.0 %all-to-all-done = bf16[32,40,1024]{2,1,0:T(8,128)(2,1)} async-done(((bf16[32,40,1024]{2,1,0:T(8,128)(2,1)}), bf16[32,40,1024]{2,1,0:T(8,128)(2,1)}, u32[]{:S(2)}, u32[]{:S(2)}) %all-to-all-start) | async-done | bytes 2621472 | tf_op jit(solution)/shard_map/all_to_all | solution.py:59
  101.0 2.3 collective-permute-done.5.refs_2_
  107.8 7.0 %project_down.1 = (bf16[768,640]{1,0:T(8,128)(2,1)}, bf16[640,2048]{1,0:T(8,128)(2,1)}) custom-call(s32[3]{0:T(128)} %copy-done.14, bf16[1280,1024]{1,0:T(8,128)(2,1)} %bitcast.7.own, bf16[640,1024]{1,0:T(8,128)(2,1)} %copy-done.23, bf16[192,2048]{1,0:T(8,128)(2,1)} %bitcast.31, bf16[192,2048]{1,0:T(8,128)(2,1)} %copy-done.26, bf16[192,2048]{1,0:T(8,128)(2,1)} %copy-done.27, ...), custom_call_target="tpu_custom_call" | custom-call | flops 1 | bytes 30000 | tf_op jit(solution)/shard_map/project_down/pallas_call | solution.py:222
  114.7 2.2 collective-permute-start.8
  117.0 25.1 %collective-permute-done.9.theirs = bf16[1536,640]{1,0:T(8,128)(2,1)S(1)} collective-permute-done((bf16[1536,640]{1,0:T(8,128)(2,1)}, bf16[1536,640]{1,0:T(8,128)(2,1)S(1)}, u32[]{:S(2)}, u32[]{:S(2)}) %collective-permute-start.9) | collective-permute-done | bytes 1966112 | tf_op jit(solution)/shard_map/ppermute | solution.py:42
  143.4 6.9 %hidden_and_down.1 = (bf16[768,640]{1,0:T(8,128)(2,1)}, bf16[768,640]{1,0:T(8,128)(2,1)}, bf16[384,640]{1,0:T(8,128)(2,1)}, bf16[96,2048]{1,0:T(8,128)(2,1)}, bf...) custom-call(bf16[1536,640]{1,0:T(8,128)(2,1)} %get-tuple-element.57.ours, ...), custom_call_target="tpu_custom_call" | custom-call | flops 1 | bytes 30000 | tf_op jit(solution)/shard_map/hidden_and_down/pallas_call | solution.py:246
  154.7 4.6 %down_here.1 = (f32[192,2048]{1,0:T(8,128)}, bf16[192,2048]{1,0:T(8,128)(2,1)}) custom-call(bf16[384,640]{1,0:T(8,128)(2,1)} %get-tuple-element.63.rows, bf16[640,2048]{1,0:T(8,128)(2,1)} %get-tuple-element.60.dy.x, bf16[96,2048]{1,0:T(8,128)(2,1)} %copy-done.29, bf16[96,2048]{1,0:T(8,128)(2,1)} %copy-done.30, bf16[96,2048]{1,0:T(8,128)(2,1)} %copy-done.31, ...), custom_call_target="tpu_custom_call" | custom-call | flops 1 | bytes 30000 | tf_op jit(solution)/shard_map/down_here/pallas_call | solution.py:246
  159.2 3.8 %collective-permute-done.8.theirs = bf16[768,640]{1,0:T(8,128)(2,1)S(1)} collective-permute-done((bf16[768,640]{1,0:T(8,128)(2,1)}, bf16[768,640]{1,0:T(8,128)(2,1)S(1)}, u32[]{:S(2)}, u32[]{:S(2)}) %collective-permute-start.8) | collective-permute-done | bytes 983072 | tf_op jit(solution)/shard_map/ppermute | solution.py:42
  164.0 14.1 %back_products.1 = (bf16[320,1024]{1,0:T(8,128)(2,1)}, bf16[320,1024]{1,0:T(8,128)(2,1)}, bf16[1280,1024]{1,0:T(8,128)(2,1)}, bf16[96,2048]{1,0:T(8,128)(2,1)}, ...) custom-call(s32[3]{0:T(128)} %copy-done.14, ...), custom_call_target="tpu_custom_call" | custom-call | flops 1 | bytes 30000 | tf_op jit(solution)/shard_map/back_products/pallas_call | solution.py:362
  185.4 9.0 %all-to-all-start.2 = ((bf16[32,40,1024]{2,1,0:T(8,128)(2,1)}), bf16[32,40,1024]{2,1,0:T(8,128)(2,1)}, u32[]{:S(2)}, u32[]{:S(2)}) async-start(bf16[32,40,1024]{2,1,0:T(8,128)(2,1)} %bitcast.43), calls=%async_computation.2 | async-start | bytes 5242880 | tf_op jit(solution)/shard_map/all_to_all | solution.py:59
  194.5 2.1 convert_add_fusion.refs_0_
  196.6 41.7 %collective-permute-done.22.refs_1_ = bf16[384,2048]{1,0:T(8,128)(2,1)S(1)} collective-permute-done((bf16[384,2048]{1,0:T(8,128)(2,1)}, bf16[384,2048]{1,0:T(8,128)(2,1)S(1)}, u32[]{:S(2)}, u32[]{:S(2)}) %collective-permute-start.22) | collective-permute-done | bytes 1572896 | tf_op jit(solution)/shard_map/ppermute | solution.py:42
  240.3 4.9 %adam_gate_up.1 = (bf16[384,2048]{1,0:T(8,128)(2,1)}, f32[384,2048]{1,0:T(8,128)}, f32[384,2048]{1,0:T(8,128)}) custom-call(bf16[384,2048]{1,0:T(8,128)(2,1)S(1)} %bitcast.30, f32[384,2048]{1,0:T(8,128)S(1)} %bitcast.41, f32[384,2048]{1,0:T(8,128)S(1)} %bitcast.42, f32[384,2048]{1,0:T(8,128)S(1)} %convert_add_fusion.refs_0_, ...), custom_call_target="tpu_custom_call" | custom-call | flops 4999999913984 | bytes 1 | tf_op jit(solution)/shard_map/adam_gate_up/pallas_call | solution.py:397
  245.3 2.8 %fusion = f32[256,1024]{1,0:T(8,128)S(1)} fusion(bf16[1280,256]{1,0:T(8,128)(2,1)S(1)} %copy-done.13, bf16[1280,1024]{1,0:T(8,128)(2,1)} %bitcast.13), kind=kOutput, calls=%fused_computation.7 | convolution fusion | flops 671088640 | bytes 4325376 | tf_op jit(solution)/shard_map/dot_general | solution.py:70
  249.8 2.9 %adam_down.1 = (bf16[192,2048]{1,0:T(8,128)(2,1)}, f32[192,2048]{1,0:T(8,128)}, f32[192,2048]{1,0:T(8,128)}) custom-call(bf16[192,2048]{1,0:T(8,128)(2,1)S(1)} %bitcast.34, f32[192,2048]{1,0:T(8,128)S(1)} %bitcast.36, f32[192,2048]{1,0:T(8,128)S(1)} %bitcast.37, f32[192,2048]{1,0:T(8,128)S(1)} %copy-done.9, bf16[192,2048]{1,0:T(8,128)(2,1)S(1)} %copy-done.11), custom_call_target="tpu_custom_call" | custom-call | flops 1 | bytes 1 | tf_op jit(solution)/shard_map/adam_down/pallas_call | solution.py:397
  252.7 4.5 %collective-permute-done.23 = bf16[128,1024]{1,0:T(8,128)(2,1)S(1)} collective-permute-done((bf16[128,1024]{1,0:T(8,128)(2,1)S(1)}, bf16[128,1024]{1,0:T(8,128)(2,1)S(1)}, u32[]{:S(2)}, u32[]{:S(2)}) %collective-permute-start.23) | collective-permute-done | bytes 262176 | tf_op jit(solution)/shard_map/ppermute | solution.py:42
  (115 shorter events, 35.4 us)
Async XLA Ops:
  0.6 51.6 %collective-permute-start = (bf16[384,2048]{1,0:T(8,128)(2,1)}, bf16[384,2048]{1,0:T(8,128)(2,1)}, u32[]{:S(2)}, u32[]{:S(2)}) collective-permute-start(bf16[384,2048]{1,0:T(8,128)(2,1)} %bitcast.26), channel_id=1, source_target_pairs={{0,2},{1,3},{2,0},{3,1},{4,6},{5,7},{6,4},{7,5},{8,10},{9,11},{10,... | collective-permute-start | bytes 4718600 | tf_op jit(solution)/shard_map/ppermute | solution.py:42
  9.2 48.0 %all-to-all-start.1 = ((bf16[32,40,1024]{2,1,0:T(8,128)(2,1)}), bf16[32,40,1024]{2,1,0:T(8,128)(2,1)}, u32[]{:S(2)}, u32[]{:S(2)}) async-start(bf16[32,40,1024]{2,1,0:T(8,128)(2,1)} %bitcast.35), calls=%async_computation.1 | async-start | bytes 5242880 | tf_op jit(solution)/shard_map/all_to_all | solution.py:59
  52.2 4.1 %collective-permute-start.1 = (bf16[384,2048]{1,0:T(8,128)(2,1)}, bf16[384,2048]{1,0:T(8,128)(2,1)}, u32[]{:S(2)}, u32[]{:S(2)}) collective-permute-start(bf16[384,2048]{1,0:T(8,128)(2,1)} %collective-permute-done.refs_2_.part1), channel_id=1, source_target_pairs={{0,1},{1,0},{2,3},{3,2},{4,5},{5,4},{6,7},{7,6},{8,9},{9,8},{10,11... | collective-permute-start | bytes 4718600 | tf_op jit(solution)/shard_map/ppermute | solution.py:42
  57.3 41.8 %all-to-all-start = ((bf16[32,40,1024]{2,1,0:T(8,128)(2,1)}), bf16[32,40,1024]{2,1,0:T(8,128)(2,1)}, u32[]{:S(2)}, u32[]{:S(2)}) async-start(bf16[32,40,1024]{2,1,0:T(8,128)(2,1)} %bitcast.6), calls=%async_computation | async-start | bytes 5242880 | tf_op jit(solution)/shard_map/all_to_all | solution.py:59
  65.2 4.3 %collective-permute-start.3 = (bf16[384,2048]{1,0:T(8,128)(2,1)S(1)}, bf16[384,2048]{1,0:T(8,128)(2,1)S(1)}, u32[]{:S(2)}, u32[]{:S(2)}) collective-permute-start(bf16[384,2048]{1,0:T(8,128)(2,1)S(1)} %bitcast.29), channel_id=1, source_target_pairs={{0,1},{1,0},{2,3},{3,2},{4,5},{5,4},{6,7},{7,6},{8,9},{9,8},{10,11... | collective-permute-start | bytes 4718600 | tf_op jit(solution)/shard_map/ppermute | solution.py:42
  67.3 3.5 %collective-permute-start.2 = (bf16[640,1024]{1,0:T(8,128)(2,1)S(1)}, bf16[640,1024]{1,0:T(8,128)(2,1)S(1)}, u32[]{:S(2)}, u32[]{:S(2)}) collective-permute-start(bf16[640,1024]{1,0:T(8,128)(2,1)S(1)} %bitcast.44), channel_id=1, source_target_pairs={{0,1},{1,0},{2,3},{3,2},{4,5},{5,4},{6,7},{7,6},{8,9},{9,8},{10,11... | collective-permute-start | bytes 3932168 | tf_op jit(solution)/shard_map/ppermute | solution.py:42
  67.4 35.9 %collective-permute-start.5 = (bf16[192,2048]{1,0:T(8,128)(2,1)S(1)}, bf16[192,2048]{1,0:T(8,128)(2,1)S(1)}, u32[]{:S(2)}, u32[]{:S(2)}) collective-permute-start(bf16[192,2048]{1,0:T(8,128)(2,1)S(1)} %bitcast.32), channel_id=1, source_target_pairs={{0,2},{1,3},{2,0},{3,1},{4,6},{5,7},{6,4},{7,5},{8,10},{9,11},{10,... | collective-permute-start | bytes 2359304 | tf_op jit(solution)/shard_map/ppermute | solution.py:42
  83.4 58.6 %collective-permute-start.9 = (bf16[1536,640]{1,0:T(8,128)(2,1)}, bf16[1536,640]{1,0:T(8,128)(2,1)S(1)}, u32[]{:S(2)}, u32[]{:S(2)}) collective-permute-start(bf16[1536,640]{1,0:T(8,128)(2,1)} %get-tuple-element.57.ours), channel_id=1, source_target_pairs={{0,4},{4,0},{8,12},{12,8},{16,20},{20,16},{24,28},{28,24},{32,36},... | collective-permute-start | bytes 5898248 | tf_op jit(solution)/shard_map/ppermute | solution.py:42
  100.4 5.4 %collective-permute-start.4 = (bf16[640,1024]{1,0:T(8,128)(2,1)S(1)}, bf16[640,1024]{1,0:T(8,128)(2,1)S(1)}, u32[]{:S(2)}, u32[]{:S(2)}) collective-permute-start(bf16[640,1024]{1,0:T(8,128)(2,1)S(1)} %slice.17), channel_id=1, source_target_pairs={{0,1},{1,0},{2,3},{3,2},{4,5},{5,4},{6,7},{7,6},{8,9},{9,8},{10,11... | collective-permute-start | bytes 3932168 | tf_op jit(solution)/shard_map/ppermute | solution.py:42
  100.5 4.1 %collective-permute-start.6 = (bf16[192,2048]{1,0:T(8,128)(2,1)S(1)}, bf16[192,2048]{1,0:T(8,128)(2,1)S(1)}, u32[]{:S(2)}, u32[]{:S(2)}) collective-permute-start(bf16[192,2048]{1,0:T(8,128)(2,1)S(1)} %bitcast.33), channel_id=1, source_target_pairs={{0,1},{1,0},{2,3},{3,2},{4,5},{5,4},{6,7},{7,6},{8,9},{9,8},{10,11... | collective-permute-start | bytes 2359304 | tf_op jit(solution)/shard_map/ppermute | solution.py:42
  114.7 48.3 %collective-permute-start.8 = (bf16[768,640]{1,0:T(8,128)(2,1)}, bf16[768,640]{1,0:T(8,128)(2,1)S(1)}, u32[]{:S(2)}, u32[]{:S(2)}) collective-permute-start(bf16[768,640]{1,0:T(8,128)(2,1)} %get-tuple-element.59.ours), channel_id=1, source_target_pairs={{0,4},{4,0},{8,12},{12,8},{16,20},{20,16},{24,28},{28,24},{32,36},... | collective-permute-start | bytes 2949128 | tf_op jit(solution)/shard_map/ppermute | solution.py:42
  150.3 2.5 collective-permute-start.11
  150.8 2.5 collective-permute-start.12
  150.9 3.0 %collective-permute-start.13 = (bf16[96,2048]{1,0:T(8,128)(2,1)}, bf16[96,2048]{1,0:T(8,128)(2,1)S(1)}, u32[]{:S(2)}, u32[]{:S(2)}) collective-permute-start(bf16[96,2048]{1,0:T(8,128)(2,1)} %get-tuple-element.67), channel_id=1, source_target_pairs={{0,1},{1,0},{2,3},{3,2},{4,5},{5,4},{6,7},{7,6},{8,9},{9,8},{10,11... | collective-permute-start | bytes 1179656 | tf_op jit(solution)/shard_map/ppermute | solution.py:42
  159.2 21.3 %collective-permute-start.16 = (bf16[192,2048]{1,0:T(8,128)(2,1)}, bf16[192,2048]{1,0:T(8,128)(2,1)S(1)}, u32[]{:S(2)}, u32[]{:S(2)}) collective-permute-start(bf16[192,2048]{1,0:T(8,128)(2,1)} %get-tuple-element.76), channel_id=1, source_target_pairs={{0,2},{1,3},{2,0},{3,1},{4,6},{5,7},{6,4},{7,5},{8,10},{9,11},{10,... | collective-permute-start | bytes 2359304 | tf_op jit(solution)/shard_map/ppermute | solution.py:42
  178.2 3.2 %collective-permute-start.15 = (bf16[320,1024]{1,0:T(8,128)(2,1)}, bf16[320,1024]{1,0:T(8,128)(2,1)S(1)}, u32[]{:S(2)}, u32[]{:S(2)}) collective-permute-start(bf16[320,1024]{1,0:T(8,128)(2,1)} %get-tuple-element.75), channel_id=1, source_target_pairs={{0,1},{1,0},{2,3},{3,2},{4,5},{5,4},{6,7},{7,6},{8,9},{9,8},{10,11... | collective-permute-start | bytes 1966088 | tf_op jit(solution)/shard_map/ppermute | solution.py:42
  178.7 4.7 %collective-permute-start.18 = (bf16[96,2048]{1,0:T(8,128)(2,1)}, bf16[96,2048]{1,0:T(8,128)(2,1)S(1)}, u32[]{:S(2)}, u32[]{:S(2)}) collective-permute-start(bf16[96,2048]{1,0:T(8,128)(2,1)} %get-tuple-element.83), channel_id=1, source_target_pairs={{0,1},{1,0},{2,3},{3,2},{4,5},{5,4},{6,7},{7,6},{8,9},{9,8},{10,11... | collective-permute-start | bytes 1179656 | tf_op jit(solution)/shard_map/ppermute | solution.py:42
  178.8 4.6 %collective-permute-start.19 = (bf16[96,2048]{1,0:T(8,128)(2,1)}, bf16[96,2048]{1,0:T(8,128)(2,1)S(1)}, u32[]{:S(2)}, u32[]{:S(2)}) collective-permute-start(bf16[96,2048]{1,0:T(8,128)(2,1)} %get-tuple-element.84), channel_id=1, source_target_pairs={{0,1},{1,0},{2,3},{3,2},{4,5},{5,4},{6,7},{7,6},{8,9},{9,8},{10,11... | collective-permute-start | bytes 1179656 | tf_op jit(solution)/shard_map/ppermute | solution.py:42
  180.5 2.9 %collective-permute-start.20 = (bf16[96,2048]{1,0:T(8,128)(2,1)}, bf16[96,2048]{1,0:T(8,128)(2,1)S(1)}, u32[]{:S(2)}, u32[]{:S(2)}) collective-permute-start(bf16[96,2048]{1,0:T(8,128)(2,1)} %get-tuple-element.85), channel_id=1, source_target_pairs={{0,1},{1,0},{2,3},{3,2},{4,5},{5,4},{6,7},{7,6},{8,9},{9,8},{10,11... | collective-permute-start | bytes 1179656 | tf_op jit(solution)/shard_map/ppermute | solution.py:42
  180.5 3.2 %collective-permute-start.21 = (bf16[96,2048]{1,0:T(8,128)(2,1)}, bf16[96,2048]{1,0:T(8,128)(2,1)S(1)}, u32[]{:S(2)}, u32[]{:S(2)}) collective-permute-start(bf16[96,2048]{1,0:T(8,128)(2,1)} %get-tuple-element.86), channel_id=1, source_target_pairs={{0,1},{1,0},{2,3},{3,2},{4,5},{5,4},{6,7},{7,6},{8,9},{9,8},{10,11... | collective-permute-start | bytes 1179656 | tf_op jit(solution)/shard_map/ppermute | solution.py:42
  183.3 11.2 %collective-permute-start.17 = (bf16[384,2048]{1,0:T(8,128)(2,1)}, bf16[384,2048]{1,0:T(8,128)(2,1)}, u32[]{:S(2)}, u32[]{:S(2)}) collective-permute-start(bf16[384,2048]{1,0:T(8,128)(2,1)} %get-tuple-element.81), channel_id=1, source_target_pairs={{0,1},{1,0},{2,3},{3,2},{4,5},{5,4},{6,7},{7,6},{8,9},{9,8},{10,11... | collective-permute-start | bytes 4718600 | tf_op jit(solution)/shard_map/ppermute | solution.py:42
  185.4 53.0 %collective-permute-start.22 = (bf16[384,2048]{1,0:T(8,128)(2,1)}, bf16[384,2048]{1,0:T(8,128)(2,1)S(1)}, u32[]{:S(2)}, u32[]{:S(2)}) collective-permute-start(bf16[384,2048]{1,0:T(8,128)(2,1)} %add_convert_fusion), channel_id=1, source_target_pairs={{0,2},{1,3},{2,0},{3,1},{4,6},{5,7},{6,4},{7,5},{8,10},{9,11},{10,... | collective-permute-start | bytes 4718600 | tf_op jit(solution)/shard_map/ppermute | solution.py:42
  185.4 59.8 %all-to-all-start.2 = ((bf16[32,40,1024]{2,1,0:T(8,128)(2,1)}), bf16[32,40,1024]{2,1,0:T(8,128)(2,1)}, u32[]{:S(2)}, u32[]{:S(2)}) async-start(bf16[32,40,1024]{2,1,0:T(8,128)(2,1)} %bitcast.43), calls=%async_computation.2 | async-start | bytes 5242880 | tf_op jit(solution)/shard_map/all_to_all | solution.py:59
  248.1 9.1 %collective-permute-start.23 = (bf16[128,1024]{1,0:T(8,128)(2,1)S(1)}, bf16[128,1024]{1,0:T(8,128)(2,1)S(1)}, u32[]{:S(2)}, u32[]{:S(2)}) collective-permute-start(bf16[128,1024]{1,0:T(8,128)(2,1)S(1)} %select_convert_fusion), channel_id=1, source_target_pairs={{0,2},{1,3},{2,0},{3,1},{4,6},{5,7},{6,4},{7,5},{8,10},{9,11},{10,... | collective-permute-start | bytes 786440 | tf_op jit(solution)/shard_map/ppermute | solution.py:42
  (36 other events, 340.7 us)
